TPU v7x, 32 devices: a whole 2x2x4 slice. The times are simulated.
32 devices in a mesh: batch: 4 (over y, x), seq: 8 (over z, core).
Axes of the slice: x: 2, y: 2, z: 4, core: 2. Of those that a mesh axis runs over, the one named last changes fastest.
Arguments:
- inputs: bfloat16 [4, 8192, 312], P('batch', 'seq'), may hold values from -6 to 6
- teacher_input: bfloat16 [4, 8192, 768], P('batch', 'seq'), may hold values from -6 to 6
- filled_slot_mask: int32 [4, 8192], P('batch'), may hold values 0 or 1
- seg_lengths: int32 [4, 32], P('batch'), may hold values from 1 to 511, as said below
- query_weight: bfloat16 [312, 312], replicated, may hold values from -0.3125 to 0.3125
- key_weight: bfloat16 [312, 312], replicated, may hold values from -0.3125 to 0.3125
- value_weight: bfloat16 [312, 312], replicated, may hold values from -0.3125 to 0.3125
- w_output: bfloat16 [312, 312], replicated, may hold values from -3.5 to 3.5
- gain_one: float32 [312], replicated, may hold values from 0.1 to 1.9
- shift_one: float32 [312], replicated, may hold values from -1.8 to 1.8
- w_inner: bfloat16 [312, 1200], replicated, may hold values from -0.3125 to 0.3125
- b_inner: float32 [1200], replicated, may hold values from -3 to 3
- w_outer: bfloat16 [1200, 312], replicated, may hold values from -0.1875 to 0.1875
- b_outer: float32 [312], replicated, may hold values from -1.8 to 1.8
- gain_two: float32 [312], replicated, may hold values from 0.1 to 1.9
- shift_two: float32 [312], replicated, may hold values from -1.8 to 1.8
- w_hidden: bfloat16 [312, 768], replicated, may hold values from -0.3125 to 0.3125
- teacher_query_weight: bfloat16 [768, 768], replicated, may hold values from -0.21875 to 0.21875
- teacher_key_weight: bfloat16 [768, 768], replicated, may hold values from -0.21875 to 0.21875
- teacher_value_weight: bfloat16 [768, 768], replicated, may hold values from -0.21875 to 0.21875
- teacher_output: bfloat16 [768, 768], replicated, may hold values from -2 to 2
- teacher_gain_one: float32 [768], replicated, may hold values from 0.1 to 1.9
- teacher_shift_one: float32 [768], replicated, may hold values from -1.8 to 1.8
- teacher_inner: bfloat16 [768, 3072], replicated, may hold values from -0.21875 to 0.21875
- teacher_outer: bfloat16 [3072, 768], replicated, may hold values from -0.109375 to 0.109375
- teacher_gain_two: float32 [768], replicated, may hold values from 0.1 to 1.9
- teacher_shift_two: float32 [768], replicated, may hold values from -1.8 to 1.8
Outputs:
- student_out: bfloat16 [4, 8192, 312], P('batch', 'seq')
- grad_inputs: bfloat16 [4, 8192, 312], P('batch', 'seq')
- loss: float32 [], replicated
- grad_w_query: float32 [312, 312], replicated
- grad_w_key: float32 [312, 312], replicated
- grad_w_value: float32 [312, 312], replicated
- grad_w_output: float32 [312, 312], replicated
- grad_gain_one: float32 [312], replicated
- grad_shift_one: float32 [312], replicated
- grad_w_inner: float32 [312, 1200], replicated
- grad_b_inner: float32 [1200], replicated
- grad_w_outer: float32 [1200, 312], replicated
- grad_b_outer: float32 [312], replicated
- grad_gain_two: float32 [312], replicated
- grad_shift_two: float32 [312], replicated
- grad_w_hidden: float32 [312, 768], replicated
Inputs may be any that keep to these rules, and one draw needn't show every extreme that they name: `seg_lengths`: the segments of a row tile its 8192 slots in order from the first. Exactly one segment starts in each aligned window of 256 slots, and no segment starts at the first slot of a device's 1024 slots except the row's first.
All inputs are finite; a program needn't handle non-finite values. No bound on the sum of `filled_slot_mask` on one device may be relied on, other than what follows from the above.
Results may differ from a plain program's by a relative error of at most 0.0095.
Values may be sent and summed in bfloat16 or wider, within the bound.
A program may use at most 384 MiB of HBM per device.

v0:
```python
from functools import partial

import jax
import jax.numpy as jnp
from jax import lax
from jax.sharding import PartitionSpec as P

HEADS = 12
HD_S = 26
HD_T = 64
QUERY_BLOCK = 512
KEY_REACH = 256


EPSILON = 1e-05
NEGATIVE = -1e30


def with_halo(shard, sides, width):
    for axis, dim in sides:
        peers, length = (lax.axis_size(axis), shard.shape[dim])
        up = [(i, (i + 1) % peers) for i in range(peers - 1)]
        down = [(j, i) for i, j in up]
        last = lax.slice_in_dim(shard, length - width, length, axis=dim)
        first = lax.slice_in_dim(shard, 0, width, axis=dim)
        before = lax.ppermute(last, axis, up)
        after = lax.ppermute(first, axis, down)
        shard = jnp.concatenate([before, shard, after], axis=dim)
    return shard


def matmul(left_side, right_side):
    return jnp.dot(left_side, right_side, preferred_element_type=jnp.float32)


def left_product(left_side, right_side):
    return lax.dot_general(
        left_side, right_side, (((0,), (0,)), ((), ())), preferred_element_type=jnp.float32
    )


def right_product(left_side, right_side):
    return lax.dot_general(
        left_side, right_side, (((1,), (1,)), ((), ())), preferred_element_type=jnp.float32
    )


def normalize(values, gain_vec, shift_vec):
    center = values - jnp.mean(values, -1, keepdims=True)
    rscale = lax.rsqrt(jnp.mean(center * center, -1, keepdims=True) + EPSILON)
    unit_rows = center * rscale
    return (unit_rows * gain_vec + shift_vec, unit_rows, rscale)


def normalize_back(grad_out, unit_rows, rscale, gain_vec):
    scaled = grad_out * gain_vec
    grad_in = rscale * (
        scaled
        - jnp.mean(scaled, -1, keepdims=True)
        - unit_rows * jnp.mean(scaled * unit_rows, -1, keepdims=True)
    )
    return (grad_in, jnp.sum(grad_out * unit_rows, 0), jnp.sum(grad_out, 0))


def split_heads(rows_in, head_width):
    return rows_in.reshape(rows_in.shape[0], HEADS, head_width)


def head_scores(query_vectors, key_rows, head_width):
    return jnp.einsum(
        "qhd,khd->hqk",
        split_heads(query_vectors, head_width),
        split_heads(key_rows, head_width),
        preferred_element_type=jnp.float32,
    ) * head_width ** (-0.5)


def first_softmax(scores, allowed):
    masked = jnp.where(allowed[None], scores, NEGATIVE)
    row_top = jnp.max(masked, -1, keepdims=True)
    weights = jnp.exp(masked - row_top)
    row_total = jnp.sum(weights, -1, keepdims=True)
    return (weights / row_total, row_top + jnp.log(row_total))


def again_softmax(scores, allowed, log_total):
    return jnp.exp(jnp.where(allowed[None], scores, NEGATIVE) - log_total)


def head_context(probabilities, value_rows, head_width):
    mixed_rows = jnp.einsum(
        "hqk,khd->qhd",
        probabilities.astype(jnp.bfloat16),
        split_heads(value_rows, head_width),
        preferred_element_type=jnp.float32,
    )
    return mixed_rows.reshape(mixed_rows.shape[0], HEADS * head_width)


def local(
    inputs,
    teacher_input,
    filled_slot_mask,
    seg_lengths,
    query_weight,
    key_weight,
    value_weight,
    w_output,
    gain_one,
    shift_one,
    w_inner,
    b_inner,
    w_outer,
    b_outer,
    gain_two,
    shift_two,
    w_hidden,
    teacher_query_weight,
    teacher_key_weight,
    teacher_value_weight,
    teacher_output,
    teacher_gain_one,
    teacher_shift_one,
    teacher_inner,
    teacher_outer,
    teacher_gain_two,
    teacher_shift_two,
):
    student_x = inputs[0]
    teacher_x = teacher_input[0]
    local_slots = student_x.shape[0]
    width_s = student_x.shape[1]
    width_t = teacher_x.shape[1]
    window = local_slots + 2 * KEY_REACH
    span = QUERY_BLOCK + 2 * KEY_REACH
    blocks = local_slots // QUERY_BLOCK
    row_slots = local_slots * lax.axis_size("seq")
    first_slot = lax.axis_index("seq") * local_slots
    slot_positions = first_slot - KEY_REACH + jnp.arange(window, dtype=jnp.int32)
    lengths = seg_lengths[0]
    start_positions = jnp.cumsum(lengths) - lengths
    seg_window = (
        jnp.sum((start_positions[None, :] <= slot_positions[:, None]).astype(jnp.int32), axis=1) - 1
    )
    seg_window = jnp.where(slot_positions < row_slots, seg_window, -1)
    mask_window = lax.dynamic_slice_in_dim(
        jnp.pad(filled_slot_mask[0], (KEY_REACH, KEY_REACH)), first_slot, window
    )
    valid_rows = mask_window[KEY_REACH : KEY_REACH + local_slots].astype(jnp.float32)
    key_index = jnp.arange(span, dtype=jnp.int32)
    own_slots = KEY_REACH + jnp.arange(QUERY_BLOCK, dtype=jnp.int32)
    s_query = matmul(student_x, query_weight).astype(jnp.bfloat16)
    s_key = matmul(student_x, key_weight).astype(jnp.bfloat16)
    s_value = matmul(student_x, value_weight).astype(jnp.bfloat16)
    teacher_query_rows = matmul(teacher_x, teacher_query_weight).astype(jnp.bfloat16)
    t_key = matmul(teacher_x, teacher_key_weight).astype(jnp.bfloat16)
    t_value = matmul(teacher_x, teacher_value_weight).astype(jnp.bfloat16)
    packed = jnp.concatenate([s_key, s_value, t_key, t_value], 1)
    widened = with_halo(packed, (("seq", 0),), KEY_REACH)
    s_key_all = widened[:, :width_s]
    s_value_all = widened[:, width_s : 2 * width_s]
    t_key_all = widened[:, 2 * width_s : 2 * width_s + width_t]
    t_value_all = widened[:, 2 * width_s + width_t :]
    masks_list = []
    t_logs = []
    s_logs = []
    t_parts = []
    s_parts = []
    attention_sum = jnp.zeros((), jnp.float32)
    for block_number in range(blocks):
        lower_row = block_number * QUERY_BLOCK
        rows_here = slice(lower_row, lower_row + QUERY_BLOCK)
        keys_here = slice(lower_row, lower_row + span)
        seg_keys = seg_window[keys_here]
        seg_query = seg_keys[KEY_REACH : KEY_REACH + QUERY_BLOCK]
        allowed = (seg_query[:, None] == seg_keys[None, :]) & (
            (mask_window[keys_here][None, :] == 1) | (own_slots[:, None] == key_index[None, :])
        )
        t_prob, t_log = first_softmax(
            head_scores(teacher_query_rows[rows_here], t_key_all[keys_here], HD_T), allowed
        )
        t_parts.append(head_context(t_prob, t_value_all[keys_here], HD_T))
        s_prob, s_log = first_softmax(
            head_scores(s_query[rows_here], s_key_all[keys_here], HD_S), allowed
        )
        s_parts.append(head_context(s_prob, s_value_all[keys_here], HD_S))
        prob_gap = s_prob - t_prob
        attention_sum = attention_sum + jnp.sum(
            valid_rows[rows_here][None, :, None] * prob_gap * prob_gap
        )
        masks_list.append(allowed)
        t_logs.append(t_log)
        s_logs.append(s_log)
    t_context = jnp.concatenate(t_parts, 0).astype(jnp.bfloat16)
    t_normed = normalize(
        teacher_x.astype(jnp.float32) + matmul(t_context, teacher_output),
        teacher_gain_one,
        teacher_shift_one,
    )[0]
    t_active = jax.nn.gelu(
        matmul(t_normed.astype(jnp.bfloat16), teacher_inner), approximate=False
    ).astype(jnp.bfloat16)
    t_target = normalize(
        t_normed + matmul(t_active, teacher_outer), teacher_gain_two, teacher_shift_two
    )[0]
    context = jnp.concatenate(s_parts, 0).astype(jnp.bfloat16)
    normed, unit_one, rscale_one = normalize(
        student_x.astype(jnp.float32) + matmul(context, w_output), gain_one, shift_one
    )
    normed_low = normed.astype(jnp.bfloat16)
    inner_pre = matmul(normed_low, w_inner) + b_inner
    activated, gelu_back = jax.vjp(partial(jax.nn.gelu, approximate=False), inner_pre)
    active_low = activated.astype(jnp.bfloat16)
    student_model, unit_two, rscale_two = normalize(
        normed + matmul(active_low, w_outer) + b_outer, gain_two, shift_two
    )
    student_low = student_model.astype(jnp.bfloat16)
    gap_hidden = matmul(student_low, w_hidden) - t_target
    local_sum = width_t * attention_sum + jnp.sum(valid_rows[:, None] * gap_hidden * gap_hidden)
    d_proj = (2.0 * valid_rows[:, None] * gap_hidden).astype(jnp.bfloat16)
    g_w_hidden = left_product(student_low, d_proj)
    d_student = right_product(d_proj, w_hidden)
    d_res_two, g_gain_two, g_shift_two = normalize_back(d_student, unit_two, rscale_two, gain_two)
    d_outer = d_res_two.astype(jnp.bfloat16)
    g_b_outer = jnp.sum(d_outer.astype(jnp.float32), 0)
    g_w_outer = left_product(active_low, d_outer)
    d_inner = gelu_back(right_product(d_outer, w_outer))[0].astype(jnp.bfloat16)
    g_b_inner = jnp.sum(d_inner.astype(jnp.float32), 0)
    g_w_inner = left_product(normed_low, d_inner)
    d_normed = right_product(d_inner, w_inner) + d_res_two
    d_res_one, g_gain_one, g_shift_one = normalize_back(d_normed, unit_one, rscale_one, gain_one)
    d_attended = d_res_one.astype(jnp.bfloat16)
    g_w_output = left_product(context, d_attended)
    d_context = right_product(d_attended, w_output).astype(jnp.bfloat16)
    score_scale = HD_S ** (-0.5)
    d_key_all = jnp.zeros((window, width_s), jnp.float32)
    d_value_all = jnp.zeros((window, width_s), jnp.float32)
    d_query_parts = []
    for block_number in range(blocks):
        lower_row = block_number * QUERY_BLOCK
        rows_here = slice(lower_row, lower_row + QUERY_BLOCK)
        keys_here = slice(lower_row, lower_row + span)
        allowed = masks_list[block_number]
        key_rows = s_key_all[keys_here]
        s_prob = again_softmax(
            head_scores(s_query[rows_here], key_rows, HD_S), allowed, s_logs[block_number]
        )
        t_prob = again_softmax(
            head_scores(teacher_query_rows[rows_here], t_key_all[keys_here], HD_T),
            allowed,
            t_logs[block_number],
        )
        grad_heads = split_heads(d_context[rows_here], HD_S)
        d_prob = jnp.einsum(
            "qhd,khd->hqk",
            grad_heads,
            split_heads(s_value_all[keys_here], HD_S),
            preferred_element_type=jnp.float32,
        )
        d_prob = d_prob + 2.0 * width_t * valid_rows[rows_here][None, :, None] * (s_prob - t_prob)
        d_score = (s_prob * (d_prob - jnp.sum(s_prob * d_prob, -1, keepdims=True))).astype(
            jnp.bfloat16
        )
        d_query_parts.append(
            jnp.einsum(
                "hqk,khd->qhd",
                d_score,
                split_heads(key_rows, HD_S),
                preferred_element_type=jnp.float32,
            ).reshape(QUERY_BLOCK, width_s)
            * score_scale
        )
        d_key_all = d_key_all.at[keys_here].add(
            jnp.einsum(
                "hqk,qhd->khd",
                d_score,
                split_heads(s_query[rows_here], HD_S),
                preferred_element_type=jnp.float32,
            ).reshape(span, width_s)
            * score_scale
        )
        d_value_all = d_value_all.at[keys_here].add(
            jnp.einsum(
                "hqk,qhd->khd",
                s_prob.astype(jnp.bfloat16),
                grad_heads,
                preferred_element_type=jnp.float32,
            ).reshape(span, width_s)
        )
    d_pair = jnp.concatenate([d_key_all, d_value_all], 1)
    rims_out = jnp.concatenate([d_pair[:KEY_REACH], d_pair[KEY_REACH + local_slots :]], 0)
    returned = with_halo(rims_out.astype(jnp.bfloat16), (("seq", 0),), KEY_REACH).astype(
        rims_out.dtype
    )
    own_pair = d_pair[KEY_REACH : KEY_REACH + local_slots]
    own_pair = own_pair.at[:KEY_REACH].add(returned[:KEY_REACH])
    own_pair = own_pair.at[local_slots - KEY_REACH :].add(returned[3 * KEY_REACH :])
    d_key = own_pair[:, :width_s].astype(jnp.bfloat16)
    d_value = own_pair[:, width_s:].astype(jnp.bfloat16)
    d_query = jnp.concatenate(d_query_parts, 0).astype(jnp.bfloat16)
    g_w_query = left_product(student_x, d_query)
    g_w_key = left_product(student_x, d_key)
    g_w_value = left_product(student_x, d_value)
    d_input = (
        right_product(d_query, query_weight)
        + right_product(d_key, key_weight)
        + right_product(d_value, value_weight)
        + d_res_one
    )
    every_token = local_slots * lax.axis_size("seq") * lax.axis_size("batch")
    summed_total = lax.psum(
        (
            g_w_query,
            g_w_key,
            g_w_value,
            g_w_output,
            g_gain_one,
            g_shift_one,
            g_w_inner,
            g_b_inner,
            g_w_outer,
            g_b_outer,
            g_gain_two,
            g_shift_two,
            g_w_hidden,
            local_sum,
        ),
        ("batch", "seq"),
    )
    return (
        student_model.astype(jnp.bfloat16)[None],
        d_input.astype(jnp.bfloat16)[None],
        summed_total[13] / (every_token * width_t),
        summed_total[0] / every_token,
        summed_total[1] / every_token,
        summed_total[2] / every_token,
        summed_total[3] / every_token,
        summed_total[4] / every_token,
        summed_total[5] / every_token,
        summed_total[6] / every_token,
        summed_total[7] / every_token,
        summed_total[8] / every_token,
        summed_total[9] / every_token,
        summed_total[10] / every_token,
        summed_total[11] / every_token,
        summed_total[12] / every_token,
    )


def solution(mesh):
    placed = (
        P("batch", "seq", None),
        P("batch", "seq", None),
        P("batch", None),
        P("batch", None),
        P(),
        P(),
        P(),
        P(),
        P(),
        P(),
        P(),
        P(),
        P(),
        P(),
        P(),
        P(),
        P(),
        P(),
        P(),
        P(),
        P(),
        P(),
        P(),
        P(),
        P(),
        P(),
        P(),
    )
    return jax.shard_map(
        local,
        mesh=mesh,
        in_specs=placed,
        out_specs=(
            P("batch", "seq", None),
            P("batch", "seq", None),
            P(),
            P(),
            P(),
            P(),
            P(),
            P(),
            P(),
            P(),
            P(),
            P(),
            P(),
            P(),
            P(),
            P(),
        ),
        check_vma=False,
    )
```

profile of v0, /device:TPU:0, one launch (start us, length us, event | category | flops | bytes accessed | tf_op | source)
XLA Modules:
  0.0 686.3 jit_solution(2156266711369523792)
XLA Ops:
  51.6 13.2 %fusion.200 = f32[12,512,1024]{2,1,0:T(8,128)} fusion(bf16[512,12,26]{0,2,1:T(8,128)(2,1)} %reshape.533, bf16[1024,12,26]{0,2,1:T(8,128)(2,1)} %reshape.534), kind=kOutput, calls=%fused_computation.317 | convolution fusion | flops 327155712 | bytes 26124288 | tf_op jit(solution)/shard_map/qhd,khd->hqk/dot_general | solution.py:70
  64.9 6.4 pad_maximum_fusion.5
  71.3 18.0 %fusion.13 = (f32[12,512]{1,0:T(8,128)S(1)}, f32[12,512]{1,0:T(8,128)S(1)}, f32[12,512,1024]{2,1,0:T(8,128)}) fusion(pred[512,1024]{1,0:T(8,128)(4,1)} %get-tuple-element.188, f32[12,512,1024]{2,1,0:T(8,128)} %fusion.200, bf16[512,12,64]{0,2,1:T(8,128)(2,1)} %bitcast.167, bf16[1024,12,64]{0,2,1:T(8,128)(2,1)} %bitcast.165), kind=kOutput, calls=%fused_computation.32 | convolution fusion | flops 843042816 | bytes 53264384 | tf_op jit(solution)/shard_map/qhd,khd->hqk/dot_general | solution.py:70
  89.3 21.8 %fusion.9 = (f32[12,512]{1,0:T(8,128)S(1)}, f32[12,512]{1,0:T(8,128)S(1)}) fusion(f32[12,512,1024]{2,1,0:T(8,128)} %get-tuple-element.191, f32[12,512]{1,0:T(8,128)S(1)} %get-tuple-element.138, pred[512,1024]{1,0:T(8,128)(4,1)} %get-tuple-element.188, f32[12,512]{1,0:T(8,128)S(1)} %get-tuple-element.139, f32[12,512,1024]{2,1,0:T(8,128)} %fusion.200), kind=kLoop, calls=%fused_computation.27 | loop fusion | flops 50319360 | bytes 50954240 | tf_op jit(solution)/shard_map/reduce_sum | solution.py:82
  111.8 13.6 %fusion.91 = bf16[12,64,512]{2,1,0:T(8,128)(2,1)} fusion(bf16[1024,12,64]{0,2,1:T(8,128)(2,1)} %bitcast.169, f32[12,512]{1,0:T(8,128)S(1)} %get-tuple-element.136, f32[12,512]{1,0:T(8,128)S(1)} %get-tuple-element.138, f32[12,512,1024]{2,1,0:T(8,128)} %get-tuple-element.191, pred[512,1024]{1,0:T(8,128)(4,1)S(1)} %copy-done.21), kind=kOutput, calls=%fused_computation.140 | convolution fusion | flops 837156864 | bytes 28098560 | tf_op jit(solution)/shard_map/hqk,khd->qhd/dot_general | solution.py:91
  126.1 8.1 %fusion.107 = bf16[512,12,26]{0,2,1:T(8,128)(2,1)} fusion(bf16[1024,12,26]{0,2,1:T(8,128)(2,1)S(1)} %copy-done.43, f32[12,512]{1,0:T(8,128)S(1)} %get-tuple-element.137, f32[12,512]{1,0:T(8,128)S(1)} %get-tuple-element.139, f32[12,512,1024]{2,1,0:T(8,128)S(1)} %bitcast.157, pred[512,1024]{1,0:T(8,128)(4,1)S(1)} %copy-done.21), kind=kOutput, calls=%fused_computation.174 | convolution fusion | flops 358772736 | bytes 26697728 | tf_op jit(solution)/shard_map/hqk,khd->qhd/dot_general | solution.py:91
  136.0 13.2 %fusion.199 = f32[12,512,1024]{2,1,0:T(8,128)} fusion(bf16[512,12,26]{0,2,1:T(8,128)(2,1)} %reshape.529, bf16[1024,12,26]{0,2,1:T(8,128)(2,1)} %reshape.530), kind=kOutput, calls=%fused_computation.316 | convolution fusion | flops 327155712 | bytes 26124288 | tf_op jit(solution)/shard_map/qhd,khd->hqk/dot_general | solution.py:70
  149.2 9.2 %pad_maximum_fusion.10 = (bf16[1024,768]{0,1:T(8,128)(2,1)}, bf16[1024,768]{0,1:T(8,128)(2,1)}) fusion(bf16[256,2160]{0,1:T(8,128)(2,1)} %collective-permute-done, bf16[1024,768]{0,1:T(8,128)(2,1)S(1)} %copy-done.5, bf16[1024,768]{0,1:T(8,128)(2,1)S(1)} %convolution_convert_fusion.2, bf16[1024,312]{0,1:T(8,128)(2,1)S(1)} %copy-done.11, ...), kind=kLoop, calls=%fused_computation.120 | loop fusion | flops 15728640 | bytes 8675328 | tf_op jit(solution)/shard_map/slice | solution.py:182
  158.4 18.0 %fusion.12 = (f32[12,512]{1,0:T(8,128)S(1)}, f32[12,512]{1,0:T(8,128)S(1)}, f32[12,512,1024]{2,1,0:T(8,128)}) fusion(pred[512,1024]{1,0:T(8,128)(4,1)} %get-tuple-element.189, f32[12,512,1024]{2,1,0:T(8,128)} %fusion.199, bf16[512,12,64]{0,2,1:T(8,128)(2,1)} %bitcast.166, bf16[1024,12,64]{0,2,1:T(8,128)(2,1)} %bitcast.164), kind=kOutput, calls=%fused_computation.31 | convolution fusion | flops 843042816 | bytes 53264384 | tf_op jit(solution)/shard_map/qhd,khd->hqk/dot_general | solution.py:70
  176.4 21.4 %fusion.7 = (f32[12,512]{1,0:T(8,128)S(1)}, f32[12,512]{1,0:T(8,128)S(1)}) fusion(f32[12,512,1024]{2,1,0:T(8,128)} %get-tuple-element.190, f32[12,512]{1,0:T(8,128)S(1)} %get-tuple-element.134, pred[512,1024]{1,0:T(8,128)(4,1)S(1)} %copy-done.23, f32[12,512]{1,0:T(8,128)S(1)} %get-tuple-element.135, f32[12,512,1024]{2,1,0:T(8,128)} %fusion.199), kind=kLoop, calls=%fused_computation.25 | loop fusion | flops 50319360 | bytes 50954240 | tf_op jit(solution)/shard_map/reduce_sum | solution.py:82
  198.6 14.0 %fusion.88 = bf16[12,64,512]{2,1,0:T(8,128)(2,1)} fusion(bf16[1024,12,64]{0,2,1:T(8,128)(2,1)S(1)} %bitcast.168, f32[12,512]{1,0:T(8,128)S(1)} %get-tuple-element.132, f32[12,512]{1,0:T(8,128)S(1)} %get-tuple-element.134, f32[12,512,1024]{2,1,0:T(8,128)} %get-tuple-element.190, pred[512,1024]{1,0:T(8,128)(4,1)S(1)} %copy-done.23), kind=kOutput, calls=%fused_computation.139 | convolution fusion | flops 837156864 | bytes 28098560 | tf_op jit(solution)/shard_map/hqk,khd->qhd/dot_general | solution.py:91
  213.3 8.3 %fusion.110 = bf16[512,12,26]{0,2,1:T(8,128)(2,1)S(1)} fusion(bf16[1024,12,26]{0,2,1:T(8,128)(2,1)} %reshape.528, f32[12,512]{1,0:T(8,128)S(1)} %get-tuple-element.133, f32[12,512]{1,0:T(8,128)S(1)} %get-tuple-element.135, f32[12,512,1024]{2,1,0:T(8,128)S(1)} %bitcast.159, pred[512,1024]{1,0:T(8,128)(4,1)S(1)} %copy-done.23), kind=kOutput, calls=%fused_computation.175 | convolution fusion | flops 358772736 | bytes 26697728 | tf_op jit(solution)/shard_map/hqk,khd->qhd/dot_general | solution.py:91
  226.8 33.0 %fusion.64.clone.4 = bf16[1024,3072]{1,0:T(8,128)(2,1)S(1)} fusion(bf16[768,3072]{1,0:T(8,128)(2,1)S(1)} %bitcast.173, f32[1024,768]{1,0:T(8,128)S(1)} %get-tuple-element.198, f32[768]{0:T(1024)S(1)} %copy-done.101, f32[768]{0:T(1024)S(1)} %copy-done.102, f32[1024]{0:T(1024)S(1)} %add_rsqrt_fusion.1, ...), kind=kOutput, calls=%fused_computation.37.clone.clone.clone.clone.clone.clone.1 | convolution fusion | flops 5040242688 | bytes 14170112 | tf_op jit(solution)/shard_map/dot_general | solution.py:33
  259.8 5.4 fusion.196
  266.8 12.1 %multiply_convert_fusion.2 = (bf16[1024,1200]{0,1:T(8,128)(2,1)S(1)}, f32[1024,1200]{0,1:T(8,128)S(1)}, f32[1024,1200]{0,1:T(8,128)S(1)}) fusion(f32[1200]{0:T(1024)S(1)} %copy-done.100, bf16[312,1200]{1,0:T(8,128)(2,1)S(1)} %copy-done.99, f32[1024,312]{0,1:T(8,128)S(1)} %copy-done.20, f32[312]{0:T(512)S(1)} %copy-done.106, f32[312]{0:T(512)S(1)} %copy-done.89, ...), kind=kOutput, calls=%fused_computation.75 | convolution fusion | flops 849469440 | bytes 14330240 | tf_op jit(solution)/shard_map/dot_general | solution.py:33
  301.3 12.4 %fusion.81 = f32[1024,12,26]{0,2,1:T(8,128)} fusion(bf16[512,12,26]{0,2,1:T(8,128)(2,1)S(1)} %reshape.544, f32[12,512]{1,0:T(8,128)S(1)} %copy-done.65, f32[12,512,1024]{2,1,0:T(8,128)} %fusion.199, pred[512,1024]{1,0:T(8,128)(4,1)S(1)} %copy-done.24), kind=kOutput, calls=%fused_computation.133 | convolution fusion | flops 352321536 | bytes 27312128 | tf_op jit(solution)/shard_map/hqk,qhd->khd/dot_general | solution.py:283
  313.8 12.5 %fusion.84 = f32[1024,12,26]{0,2,1:T(8,128)} fusion(bf16[512,12,26]{0,2,1:T(8,128)(2,1)S(1)} %reshape.545, f32[12,512]{1,0:T(8,128)S(1)} %copy-done.59, f32[12,512,1024]{2,1,0:T(8,128)} %fusion.200, pred[512,1024]{1,0:T(8,128)(4,1)S(1)} %copy-done.22), kind=kOutput, calls=%fused_computation.134 | convolution fusion | flops 352321536 | bytes 27312128 | tf_op jit(solution)/shard_map/hqk,qhd->khd/dot_general | solution.py:283
  326.5 33.6 %fusion.1 = (f32[]{:T(128)}, f32[12,512]{1,0:T(8,128)S(1)}, f32[12,512,1024]{2,1,0:T(8,128)}) fusion(f32[512]{0:T(512)S(1)} %copy-done.93, f32[12,512]{1,0:T(8,128)S(1)} %copy-done.61, f32[12,512]{1,0:T(8,128)S(1)} %copy-done.49, f32[12,512,1024]{2,1,0:T(8,128)} %get-tuple-element.191, pred[512,1024]{1,0:T(8,128)(4,1)S(1)} %copy-done.22, ...), kind=kOutput, calls=%fused_computation.3 | convolution fusion | flops 446687232 | bytes 77156352 | tf_op jit(solution)/shard_map/qhd,khd->hqk/dot_general | solution.py:254
  360.2 32.2 %fusion = (f32[]{:T(128)}, f32[12,512]{1,0:T(8,128)S(1)}, f32[12,512,1024]{2,1,0:T(8,128)}) fusion(f32[512]{0:T(512)S(1)} %copy-done.92, f32[12,512]{1,0:T(8,128)S(1)} %copy-done.67, f32[12,512]{1,0:T(8,128)S(1)} %copy-done.53, f32[12,512,1024]{2,1,0:T(8,128)} %get-tuple-element.190, pred[512,1024]{1,0:T(8,128)(4,1)S(1)} %copy-done.24, ...), kind=kOutput, calls=%fused_computation.2 | convolution fusion | flops 446687232 | bytes 77156352 | tf_op jit(solution)/shard_map/qhd,khd->hqk/dot_general | solution.py:254
  392.4 57.7 %multiply_convert_fusion = (bf16[12,512,1024]{2,1,0:T(8,128)(2,1)}, bf16[12,512,1024]{2,1,0:T(8,128)(2,1)}) fusion(f32[12,512,1024]{2,1,0:T(8,128)} %get-tuple-element.204, f32[12,512,1024]{2,1,0:T(8,128)} %get-tuple-element.191, f32[12,512]{1,0:T(8,128)S(1)} %get-tuple-element.121, f32[12,512]{1,0:T(8,128)S(1)} %copy-done.58, f32[512]{0:T(512)S(1)} %copy-done.84, ...), kind=kLoop, calls=%fused_computation.4 | loop fusion | flops 150994944 | bytes 177360896 | tf_op jit(solution)/shard_map/convert_element_type | solution.py:261
  450.2 8.6 %fusion.105 = bf16[512,12,26]{0,2,1:T(8,128)(2,1)S(1)} fusion(bf16[1024,12,26]{0,2,1:T(8,128)(2,1)S(1)} %copy-done.18, bf16[12,512,1024]{2,1,0:T(8,128)(2,1)} %get-tuple-element.209), kind=kOutput, calls=%fused_computation.172 | convolution fusion | flops 327475200 | bytes 13541376 | tf_op jit(solution)/shard_map/hqk,khd->qhd/dot_general | solution.py:265
  458.8 8.1 %multiply_bitcast_fusion = f32[1024,12,26]{0,2,1:T(8,128)} fusion(bf16[512,12,26]{0,2,1:T(8,128)(2,1)S(1)} %copy-done.26, bf16[12,512,1024]{2,1,0:T(8,128)(2,1)} %get-tuple-element.209), kind=kOutput, calls=%fused_computation.127 | convolution fusion | flops 327475200 | bytes 14180352 | tf_op jit(solution)/shard_map/hqk,qhd->khd/dot_general | solution.py:274
  502.1 47.0 %all-reduce.3 = (f32[]{:T(128)}, f32[312]{0:T(512)S(1)}, f32[312]{0:T(512)S(1)}, f32[1200]{0:T(1024)S(1)}, f32[312]{0:T(512)S(1)}, /*index=5*/f32[312]{0:T(512)S(1)}, f32[312]{0:T(512)S(1)}) all-reduce(f32[]{:T(128)S(6)} %add.290, f32[312]{0:T(512)S(1)} %copy-done.90, ...), channel_id=1, replica_groups=mesh['batch'=4,'seq'=8] {'batch','seq'}, use_global_device_ids=true, to_apply=%region_27.28 | all-reduce | flops 2761 | bytes 22088 | tf_op jit(solution)/shard_map/psum | solution.py:311
  556.9 108.6 %all-reduce.7.cloned.1.call-done = (f32[312,312]{0,1:T(8,128)}, f32[312,312]{0,1:T(8,128)}, f32[312,312]{0,1:T(8,128)}, f32[312,312]{0,1:T(8,128)}, f32[312,1200...) async-done(((f32[312,312]{0,1:T(8,128)}, f32[312,312]{0,1:T(8,128)}, f32[312,312]{0,1:T(8,128)}, f32[312,312]{0,1:T(8,128)}, f32[312,1200]{1,0:T(8,128)}, ...) | async-done | bytes 5511184 | tf_op jit(solution)/shard_map/psum | solution.py:311
  (393 shorter events, 129.9 us)
Async XLA Ops:
  7.2 217.1 %copy-start = (bf16[768,768]{1,0:T(8,128)(2,1)S(1)}, bf16[768,768]{1,0:T(8,128)(2,1)}, u32[]{:S(2)}) copy-start(bf16[768,768]{1,0:T(8,128)(2,1)} %param.59) | copy-start | bytes 3538948
  7.2 658.4 %all-reduce.7.cloned.1.call-start = ((), (), s32[]{:S(2)}) async-start(), calls=%async_computation | async-start | bytes 12140544 | tf_op jit(solution)/shard_map/psum | solution.py:311
  17.5 27.4 %collective-permute-start.1 = (bf16[256,2160]{0,1:T(8,128)(2,1)}, bf16[256,2160]{0,1:T(8,128)(2,1)}, u32[]{:S(2)}, u32[]{:S(2)}) collective-permute-start(bf16[256,2160]{0,1:T(8,128)(2,1)} %get-tuple-element.168), channel_id=1, source_target_pairs={{1,0},{2,1},{3,2},{4,3},{5,4},{6,5},{7,6},{9,8},{10,9},{11,10},{12... | collective-permute-start | bytes 3317768 | tf_op jit(solution)/shard_map/ppermute | solution.py:27
  18.8 19.6 %collective-permute-start = (bf16[256,2160]{0,1:T(8,128)(2,1)}, bf16[256,2160]{0,1:T(8,128)(2,1)}, u32[]{:S(2)}, u32[]{:S(2)}) collective-permute-start(bf16[256,2160]{0,1:T(8,128)(2,1)} %get-tuple-element.169), channel_id=1, source_target_pairs={{0,1},{1,2},{2,3},{3,4},{4,5},{5,6},{6,7},{8,9},{9,10},{10,11},{11... | collective-permute-start | bytes 3317768 | tf_op jit(solution)/shard_map/ppermute | solution.py:26
  89.3 36.7 %copy-start.50 = (f32[12,512]{1,0:T(8,128)}, f32[12,512]{1,0:T(8,128)S(1)}, u32[]{:S(2)}) copy-start(f32[12,512]{1,0:T(8,128)S(1)} %get-tuple-element.139) | copy-start | bytes 73732
  89.3 36.7 %slice-start = ((s8[25165824]{0:T(1024)(128)(4,1)}), s8[4194304]{0:T(1024)(128)(4,1)S(1)}, s32[]{:S(2)}) async-start(s8[25165824]{0:T(1024)(128)(4,1)} %bitcast.156), calls=%async_computation.1 | async-start | bytes 8388608
  89.3 36.7 %slice-start.1 = ((s8[25165824]{0:T(1024)(128)(4,1)}), s8[4194304]{0:T(1024)(128)(4,1)S(1)}, s32[]{:S(2)}) async-start(s8[25165824]{0:T(1024)(128)(4,1)} %bitcast.156), calls=%async_computation.2 | async-start | bytes 8388608
  176.4 36.8 %copy-start.54 = (f32[12,512]{1,0:T(8,128)}, f32[12,512]{1,0:T(8,128)S(1)}, u32[]{:S(2)}) copy-start(f32[12,512]{1,0:T(8,128)S(1)} %get-tuple-element.135) | copy-start | bytes 73732
  176.4 36.8 %slice-start.6 = ((s8[25165824]{0:T(1024)(128)(4,1)}), s8[4194304]{0:T(1024)(128)(4,1)S(1)}, s32[]{:S(2)}) async-start(s8[25165824]{0:T(1024)(128)(4,1)} %bitcast.158), calls=%async_computation.7 | async-start | bytes 8388608
  176.4 36.8 %slice-start.7 = ((s8[25165824]{0:T(1024)(128)(4,1)}), s8[4194304]{0:T(1024)(128)(4,1)S(1)}, s32[]{:S(2)}) async-start(s8[25165824]{0:T(1024)(128)(4,1)} %bitcast.158), calls=%async_computation.8 | async-start | bytes 8388608
  313.8 46.3 %slice-start.12 = ((s8[25165824]{0:T(1024)(128)(4,1)}), s8[4194304]{0:T(1024)(128)(4,1)S(1)}, s32[]{:S(2)}) async-start(s8[25165824]{0:T(1024)(128)(4,1)} %bitcast.160), calls=%async_computation.13 | async-start | bytes 8388608
  326.4 33.7 %slice-start.13 = ((s8[25165824]{0:T(1024)(128)(4,1)}), s8[4194304]{0:T(1024)(128)(4,1)S(1)}, s32[]{:S(2)}) async-start(s8[25165824]{0:T(1024)(128)(4,1)} %bitcast.160), calls=%async_computation.14 | async-start | bytes 8388608
  326.4 33.7 %slice-start.14 = ((s8[25165824]{0:T(1024)(128)(4,1)}), s8[4194304]{0:T(1024)(128)(4,1)S(1)}, s32[]{:S(2)}) async-start(s8[25165824]{0:T(1024)(128)(4,1)} %bitcast.160), calls=%async_computation.15 | async-start | bytes 8388608
  326.4 33.7 %slice-start.15 = ((s8[25165824]{0:T(1024)(128)(4,1)}), s8[4194304]{0:T(1024)(128)(4,1)S(1)}, s32[]{:S(2)}) async-start(s8[25165824]{0:T(1024)(128)(4,1)} %bitcast.160), calls=%async_computation.16 | async-start | bytes 8388608
  392.4 57.7 %copy-start.18 = (bf16[1024,12,26]{0,2,1:T(8,128)(2,1)S(1)}, bf16[1024,12,26]{0,2,1:T(8,128)(2,1)}, u32[]{:S(2)}) copy-start(bf16[1024,12,26]{0,2,1:T(8,128)(2,1)} %reshape.534) | copy-start | bytes 1916932
  489.6 6.6 collective-permute-start.2
  493.2 3.6 collective-permute-start.3
  499.9 52.1 %copy-start.7 = (f32[1024,312]{0,1:T(8,128)S(1)}, f32[1024,312]{0,1:T(8,128)}, u32[]{:S(2)}) copy-start(f32[1024,312]{0,1:T(8,128)} %copy-done.6) | copy-start | bytes 3833860
  499.9 52.1 %copy-start.57 = (f32[1024]{0:T(1024)S(1)}, f32[1024]{0:T(1024)}, u32[]{:S(2)}) copy-start(f32[1024]{0:T(1024)} %copy-done.56) | copy-start | bytes 12292
  500.0 52.1 %copy-start.72 = (f32[1024]{0:T(1024)S(1)}, f32[1024]{0:T(1024)}, u32[]{:S(2)}) copy-start(f32[1024]{0:T(1024)} %copy-done.71) | copy-start | bytes 12292
  500.0 52.1 %copy-start.77 = (f32[312]{0:T(512)S(1)}, f32[312]{0:T(512)}, u32[]{:S(2)}) copy-start(f32[312]{0:T(512)} %param.53) | copy-start | bytes 3748
  500.0 52.1 %copy-start.88 = (f32[312]{0:T(512)S(1)}, f32[312]{0:T(512)}, u32[]{:S(2)}) copy-start(f32[312]{0:T(512)} %param.54) | copy-start | bytes 3748
  500.0 53.2 %copy-start.40 = (bf16[312,312]{1,0:T(8,128)(2,1)S(1)}, bf16[312,312]{1,0:T(8,128)(2,1)}, u32[]{:S(2)}) copy-start(bf16[312,312]{1,0:T(8,128)(2,1)} %param.43) | copy-start | bytes 584068
  500.0 53.7 %copy-start.41 = (bf16[312,312]{1,0:T(8,128)(2,1)S(1)}, bf16[312,312]{1,0:T(8,128)(2,1)}, u32[]{:S(2)}) copy-start(bf16[312,312]{1,0:T(8,128)(2,1)} %param.44) | copy-start | bytes 584068
  (114 other events, 1110.8 us)
Sparse Core Ops, SparseCore 0:
  500.1 165.3 all-reduce.6
where the time goes:
time: 692 us; the launch traced here: 686 us
  matrix products  314 us (45%)
  other arithmetic  147 us (21%)
  waiting for transfers between devices  109 us (16%)
  blocking collectives  47 us (7%)
  local copies, waits for them, and re-layouts  39.4 us (6%)
  between operations  19.9 us (3%)
  starting transfers between devices  10.4 us (2%)
    psum x1, waiting for transfers between devices, local(): lax.psum((g_w_query, g_w_key, g_w_value, g_w_output, g_gain_one, g_shift_...  109 us
    dot_general x13, matrix products, matmul(): return jnp.dot(left_side, right_side, preferred_element_type=jnp.float32)  69.4 us
    dot_general x2, matrix products, local(): jnp.einsum('qhd,khd->hqk', grad_heads, split_heads(s_value_all[keys_here]...  65.8 us
    dot_general x4, matrix products, head_scores(): jnp.einsum('qhd,khd->hqk', split_heads(query_vectors, head_width), split_...  62.5 us
    convert_element_type x1, other arithmetic, local(): (s_prob * (d_prob - jnp.sum(s_prob * d_prob, -1, keepdims=True))).astype(...  57.7 us
    psum x1, blocking collectives, local(): lax.psum((g_w_query, g_w_key, g_w_value, g_w_output, g_gain_one, g_shift_...  47 us
    dot_general x4, matrix products, head_context(): jnp.einsum('hqk,khd->qhd', probabilities.astype(jnp.bfloat16), split_head...  44 us
    reduce_sum x2, other arithmetic, first_softmax(): row_total = jnp.sum(weights, -1, keepdims=True)  43.3 us
  transfers between devices with their start and end apart: 5, of which 2 were waited for; matrix products, arithmetic and copies ran while one was open for 4% of the time, Pallas kernels for 0%

commit v1 on v0

v1 whole, which is shorter than its diff:
```python
from functools import partial

import jax
import jax.numpy as jnp
from jax import lax
from jax.experimental import pallas as pl
from jax.experimental.pallas import tpu as pltpu
from jax.sharding import PartitionSpec as P

HEADS = 12
HD_S = 26
HD_T = 64
WIN = 256
PAD = 32
SLOT_ONE = 26
PAIRS = HEADS // 2
CHUNK = 64
TAIL = 16
SLOTS = 4
BLOCK = 320
SUMS_AT = 1152
QKV_LANES = 384
MESH = pl.DeviceIdType.MESH
EPSILON = 1e-05
NEGATIVE = -1e30
LOG2E = 1.4426950408889634
F32 = jnp.float32
BF16 = jnp.bfloat16
VMEM = pl.BlockSpec(memory_space=pltpu.VMEM)
BIG = 60 << 20


def mm(left, right, dims):
    return lax.dot_general(left, right, ((dims[:1], dims[1:]), ((), ())), preferred_element_type=F32)


def nn(left, right):
    return mm(left, right, (1, 0))


def tn(left, right):
    return mm(left, right, (0, 0))


def nt(left, right):
    return mm(left, right, (1, 1))


def tt(left, right):
    return mm(left, right, (0, 1))


def pad_heads():
    row = lax.broadcasted_iota(jnp.int32, (HEADS * PAD, HEADS * HD_S), 0)
    col = lax.broadcasted_iota(jnp.int32, (HEADS * PAD, HEADS * HD_S), 1)
    spot = jnp.zeros((HEADS * PAD, HEADS * HD_S), F32)
    for head in range(HEADS):
        here = (row - head * PAD == col - head * HD_S) & (col >= head * HD_S) & (col < (head + 1) * HD_S)
        spot = jnp.where(here, 1.0, spot)
    return spot.astype(BF16)


def window_rows(mask_ref, lengths_ref, seq_index, windows, row_windows):
    lengths = lengths_ref[...].astype(F32)
    order = lax.broadcasted_iota(jnp.int32, lengths.shape, 1)
    lane = lax.broadcasted_iota(jnp.int32, (1, WIN), 1).astype(F32)
    out = []
    for j in range(windows + 2):
        number = seq_index * windows + (j - 1)
        inside = (number >= 0) & (number < row_windows)
        safe = jnp.clip(number, 0, row_windows - 1)
        start = jnp.sum(jnp.where(order < safe, lengths, 0.0), axis=1, keepdims=True)
        offset = start - (safe * WIN).astype(F32)
        late = (lane >= offset).astype(F32)
        filled = mask_ref[:, pl.ds(pl.multiple_of(safe * WIN, WIN), WIN)]
        filled = jnp.where(inside, filled.astype(F32), 0.0)
        out.append((late, filled))
    return out


def stack_rows(*rows):
    n = rows[0].shape[1]
    index = lax.broadcasted_iota(jnp.int32, (8, n), 0)
    block = jnp.zeros((8, n), F32)
    for k, row in enumerate(rows):
        block = jnp.where(index == k, row, block)
    return block.astype(BF16)


def attend_kernel(
    windows,
    row_windows,
    mask_ref,
    lengths_ref,
    xt_hbm,
    xs_ref,
    wtq_hbm,
    wtk_hbm,
    wtv_hbm,
    wq_ref,
    wk_ref,
    wv_ref,
    stats_ref,
    loss_ref,
    rows_ref,
    tctx_hbm,
    sctx_hbm,
    sq_hbm,
    skv_hbm,
    saved_e_hbm,
    saved_g_hbm,
    x_ref,
    xs_side_ref,
    wt_ref,
    bias_ref,
    wst_ref,
    tq_ref,
    tk_ref,
    tv_ref,
    sq_ref,
    skv_ref,
    tctx_ref,
    sctx_ref,
    e_ref,
    g_ref,
    work_ref,
    low_ref,
    in_sem,
    halo_send,
    halo_arrive,
    kv_sem,
    out_sem,
):
    slots = windows * WIN
    batch, seq = lax.axis_index("batch"), lax.axis_index("seq")
    peers = lax.axis_size("seq")
    has_left, has_right = seq > 0, seq < peers - 1
    width_t = x_ref.shape[1]
    extended = slots + 2 * WIN

    barrier = pltpu.get_barrier_semaphore()
    for move in (1, peers - 1):
        pl.semaphore_signal(barrier, inc=1, device_id=(batch, (seq + move) % peers), device_id_type=MESH)
    loads = [pltpu.make_async_copy(xt_hbm, x_ref.at[pl.ds(WIN, slots)], in_sem.at[0])]
    for k, w_hbm in enumerate((wtq_hbm, wtk_hbm, wtv_hbm)):
        loads.append(pltpu.make_async_copy(w_hbm, wt_ref.at[k], in_sem.at[1 + k]))
    for c in loads:
        c.start()
    pl.semaphore_wait(barrier, 2)

    def halo(side):
        device = (batch, seq - 1 + 2 * side)
        first = side * (slots - WIN)
        return [
            pltpu.make_async_remote_copy(
                src_ref=xt_hbm.at[pl.ds(first, WIN)],
                dst_ref=x_ref.at[pl.ds((1 - side) * (WIN + slots), WIN)],
                send_sem=halo_send.at[0, side],
                recv_sem=halo_arrive.at[0, 1 - side],
                device_id=device,
                device_id_type=MESH,
            ),
            pltpu.make_async_remote_copy(
                src_ref=xs_ref.at[:, pl.ds(first, WIN)],
                dst_ref=xs_side_ref.at[1 - side],
                send_sem=halo_send.at[1, side],
                recv_sem=halo_arrive.at[1, 1 - side],
                device_id=device,
                device_id_type=MESH,
            ),
        ]

    for side, present in ((0, has_left), (1, has_right)):

        @pl.when(present)
        def _():
            for c in halo(side):
                c.start()

        @pl.when(jnp.logical_not(present))
        def _():
            x_ref[side * (WIN + slots) : side * (WIN + slots) + WIN, :] = jnp.zeros((WIN, width_t), BF16)
            xs_side_ref[side] = jnp.zeros(xs_side_ref.shape[1:], BF16)

    info = window_rows(mask_ref, lengths_ref, seq, windows, row_windows)
    eye = lax.broadcasted_iota(jnp.int32, (WIN, WIN), 0) == lax.broadcasted_iota(jnp.int32, (WIN, WIN), 1)
    rows_ref[...] = jnp.zeros_like(rows_ref)
    for w in range(windows):
        late, filled = info[w + 1]
        late_l, filled_l = info[w]
        late_r, filled_r = info[w + 2]
        early = 1.0 - late
        here = slice(w * WIN, (w + 1) * WIN)
        rows_ref[0:1, here] = early
        rows_ref[1:2, here] = late
        rows_ref[2:3, here] = filled
        query = stack_rows(early, late)
        own = tn(stack_rows(NEGATIVE * (1.0 - early * filled), NEGATIVE * (1.0 - late * filled)), query)
        bias_ref[w, :WIN, :] = jnp.where(eye, 0.0, own)
        bias_ref[w, WIN:, :] = tn(
            stack_rows(
                NEGATIVE * (1.0 - late_l * filled_l), NEGATIVE * (1.0 - (1.0 - late_r) * filled_r)
            ),
            query,
        )
    loss_ref[...] = jnp.zeros_like(loss_ref)
    stats_ref[...] = jnp.zeros_like(stats_ref)
    spot = pad_heads()
    padded = HEADS * PAD
    row = lax.broadcasted_iota(jnp.int32, (padded, 1), 0) % PAD
    ones = (row >= SLOT_ONE) & (row < SLOT_ONE + 3)

    xs = xs_ref[...]
    for k, w_ref in enumerate((wq_ref, wk_ref, wv_ref)):
        wst_ref[k] = nt(spot, w_ref[...]).astype(BF16)
        made = nn(wst_ref[k], xs)
        if k == 0:
            sq_ref[...] = (made * (LOG2E * HD_S**-0.5)).astype(BF16)
        else:
            if k == 2:
                made = jnp.where(ones, 1.0, made)
            skv_ref[k - 1, :, WIN : WIN + slots] = made.astype(BF16)
    tail = (lax.broadcasted_iota(jnp.int32, (TAIL, extended), 0) == 0).astype(BF16)
    for head in range(HEADS):
        tv_ref[head * (HD_T + TAIL) + HD_T : (head + 1) * (HD_T + TAIL), :] = tail

    def put_values(made, first_head, lanes):
        for j in range(made.shape[0] // HD_T):
            at = (first_head + j) * (HD_T + TAIL)
            tv_ref[at : at + HD_T, lanes] = made[j * HD_T : (j + 1) * HD_T]

    part = width_t // 2
    loads[0].wait()
    for k in range(3):
        loads[1 + k].wait()
        for half in range(2):
            made = tt(wt_ref[k, :, half * part : (half + 1) * part], x_ref[WIN : WIN + slots, :])
            if k == 0:
                tq_ref[half * part : (half + 1) * part, :] = (made * (LOG2E * HD_T**-0.5)).astype(BF16)
            elif k == 1:
                tk_ref[half * part : (half + 1) * part, WIN : WIN + slots] = made.astype(BF16)
            else:
                put_values(made.astype(BF16), half * HEADS // 2, slice(WIN, WIN + slots))
    for side, present in ((0, has_left), (1, has_right)):

        @pl.when(present)
        def _():
            for sent, landed in zip(halo(side), halo(1 - side)):
                sent.wait_send()
                landed.wait_recv()

        lanes = slice(side * (WIN + slots), side * (WIN + slots) + WIN)
        for k in (1, 2):
            made = tt(wt_ref[k], x_ref[lanes, :]).astype(BF16)
            if k == 1:
                tk_ref[:, lanes] = made
            else:
                put_values(made, 0, lanes)
            made = nn(wst_ref[k], xs_side_ref[side])
            if k == 2:
                made = jnp.where(ones, 1.0, made)
            skv_ref[k - 1, :, lanes] = made.astype(BF16)
    finals = [
        pltpu.make_async_copy(sq_ref, sq_hbm, kv_sem.at[0]),
        pltpu.make_async_copy(skv_ref, skv_hbm, kv_sem.at[1]),
    ]
    for c in finals:
        c.start()

    def stores(pair, which):
        slot = pair % 2
        t_rows = pl.ds(pl.multiple_of(pair * 2 * HD_T, 2 * HD_T), 2 * HD_T)
        s_rows = pl.ds(pl.multiple_of(pair * 2 * PAD, 2 * PAD), 2 * PAD)
        heads = pl.ds(pair * 2, 2)
        ends = (
            (e_ref.at[slot], saved_e_hbm.at[:, heads]),
            (g_ref.at[slot], saved_g_hbm.at[:, heads]),
            (tctx_ref.at[t_rows], tctx_hbm.at[t_rows]),
            (sctx_ref.at[s_rows], sctx_hbm.at[s_rows]),
        )
        return [pltpu.make_async_copy(*ends[k], out_sem.at[k, pair]) for k in which]

    def one_pair(pair, carry):
        @pl.when(pair >= 2)
        def _():
            for c in stores(pair - 2, (0, 1)):
                c.wait()

        attend_pair(pair)
        for c in stores(pair, range(4)):
            c.start()
        return carry

    def attend_pair(pair):
        e_out, g_out = e_ref.at[pair % 2], g_ref.at[pair % 2]
        def rows_of(w):
            left = slice(w * WIN, (w + 1) * WIN)
            own = slice((w + 1) * WIN, (w + 2) * WIN)
            right = slice((w + 2) * WIN, (w + 3) * WIN)
            return left, own, right, rows_ref[0:1, left], rows_ref[1:2, left], rows_ref[2:3, left]

        def first_pass(w, q_ref, k_ref, rows, work_ref):
            left, own, right, early, late, _ = rows_of(w)
            query = q_ref[rows, left]
            query_fold = jnp.concatenate([query * early.astype(BF16), query * late.astype(BF16)], axis=0)
            keys = k_ref[rows, own]
            keys_fold = jnp.concatenate([k_ref[rows, left], k_ref[rows, right]], axis=0)
            top = None
            for part, (a, b) in enumerate(((keys, query), (keys_fold, query_fold))):
                raw = tn(a, b)
                for c in range(0, WIN, CHUNK):
                    block = raw[c : c + CHUNK] + bias_ref[w, part * WIN + c : part * WIN + c + CHUNK, :]
                    work_ref[part * WIN + c : part * WIN + c + CHUNK, :] = block
                    for r in range(0, CHUNK, 8):
                        piece = block[r : r + 8]
                        top = piece if top is None else jnp.maximum(top, piece)
            return jnp.max(top, axis=0, keepdims=True)

        def second_pass(work_ref, top, low_ref):
            for c in range(0, 2 * WIN, CHUNK):
                e = jnp.exp2(work_ref[c : c + CHUNK, :] - top)
                work_ref[c : c + CHUNK, :] = e
                low_ref[c : c + CHUNK, :] = e.astype(BF16)

        def mix(w, v_ref, rows, low_ref, head_width):
            left, own, right, early, late, _ = rows_of(w)
            values = v_ref[rows, own]
            values_fold = jnp.concatenate([v_ref[rows, left], v_ref[rows, right]], axis=0)
            mixed = nn(values, low_ref[:WIN, :])
            side = nn(values_fold, low_ref[WIN:, :])
            n = values.shape[0]
            mixed = mixed + early * side[:n] + late * side[n:]
            inverse = 1.0 / mixed[head_width : head_width + 1]
            return mixed[: -TAIL if head_width == HD_T else n] * inverse, inverse

        units = [(w, h) for w in range(windows) for h in range(2)]
        state = {}

        def refs(u):
            w, h = units[u]
            head = 2 * pair + h
            t_rows = pl.ds(pl.multiple_of(head * HD_T, HD_T), HD_T)
            s_rows = pl.ds(pl.multiple_of(head * PAD, PAD), PAD)
            v_rows = pl.ds(pl.multiple_of(head * (HD_T + TAIL), TAIL), HD_T + TAIL)
            slot = u % SLOTS
            return w, h, t_rows, s_rows, v_rows, work_ref.at[2 * slot], work_ref.at[2 * slot + 1], low_ref.at[slot]

        def score_stage(u):
            w, h, t_rows, s_rows, _, work_t, work_s, _ = refs(u)
            state[u] = [
                first_pass(w, tq_ref, tk_ref, t_rows, work_t),
                first_pass(w, sq_ref, skv_ref.at[0], s_rows, work_s),
            ]

        def power_stage(u):
            w, h, _, _, _, work_t, work_s, low_t = refs(u)
            second_pass(work_t, state[u][0], low_t)
            second_pass(work_s, state[u][1], e_out.at[w, h])

        def mix_stage(u):
            w, h, t_rows, s_rows, v_rows, _, _, low_t = refs(u)
            left = rows_of(w)[0]
            t_mixed, t_inv = mix(w, tv_ref, v_rows, low_t, HD_T)
            s_mixed, s_inv = mix(w, skv_ref.at[1], s_rows, e_out.at[w, h], SLOT_ONE)
            tctx_ref[t_rows, left] = t_mixed.astype(BF16)
            sctx_ref[s_rows, left] = s_mixed
            state[u] = [t_inv, s_inv]

        def gap_stage(u):
            w, h, _, _, _, work_t, work_s, _ = refs(u)
            left, _, _, _, _, filled = rows_of(w)
            t_inv, s_inv = state.pop(u)
            width = 2.0 * HEADS * HD_T
            scale_s = (width * filled) * s_inv * s_inv
            scale_t = (width * filled) * s_inv * t_inv
            square = jnp.zeros((8, WIN), F32)
            cross = jnp.zeros((8, WIN), F32)
            for c in range(0, 2 * WIN, CHUNK):
                s = work_s[c : c + CHUNK, :]
                gap = s * scale_s - work_t[c : c + CHUNK, :] * scale_t
                g_out[w, h, c : c + CHUNK, :] = gap.astype(BF16)
                for r in range(0, CHUNK, 8):
                    piece = gap[r : r + 8]
                    square += piece * piece
                    cross += piece * s[r : r + 8]
            square = jnp.sum(square, axis=0, keepdims=True)
            cross = jnp.sum(cross, axis=0, keepdims=True)
            back = 1.0 / (s_inv * width)
            stats_ref[pair, h : h + 1, left] = s_inv
            stats_ref[pair, 2 + h : 3 + h, left] = cross
            loss_ref[0:1, left] += square * back * back

        last = len(units)
        for u in range(last + 2):
            if u < last:
                score_stage(u)
            if 0 <= u - 1 < last:
                power_stage(u - 1)
            if 0 <= u - 2 < last:
                mix_stage(u - 2)
                gap_stage(u - 2)


    lax.fori_loop(0, PAIRS, one_pair, 0)
    for pair in range(PAIRS):
        for c in stores(pair, range(0 if pair >= PAIRS - 2 else 2, 4)):
            c.wait()
    for c in finals:
        c.wait()


def attend(mask, lengths, xt, xs, wtq, wtk, wtv, wq, wk, wv):
    slots, width_t = xt.shape
    width_s = xs.shape[0]
    windows = slots // WIN
    row_windows = mask.shape[1] // WIN
    padded = HEADS * PAD
    extended = slots + 2 * WIN
    sds = jax.ShapeDtypeStruct
    anywhere = pl.BlockSpec(memory_space=pl.ANY)
    saved = (windows, HEADS, 2 * WIN, WIN)
    return pl.pallas_call(
        partial(attend_kernel, windows, row_windows),
        out_shape=(
            sds((PAIRS, 8, slots), F32),
            sds((8, slots), F32),
            sds((8, slots), F32),
            sds((width_t, slots), BF16),
            sds((padded, slots), F32),
            sds((padded, slots), BF16),
            sds((2, padded, extended), BF16),
            sds(saved, BF16),
            sds(saved, BF16),
        ),
        in_specs=[VMEM, VMEM, anywhere, VMEM] + [anywhere] * 3 + [VMEM] * 3,
        out_specs=[VMEM] * 3 + [anywhere] * 6,
        scratch_shapes=[
            pltpu.VMEM((extended, width_t), BF16),
            pltpu.VMEM((2, width_s, WIN), BF16),
            pltpu.VMEM((3, width_t, width_t), BF16),
            pltpu.VMEM((windows, 2 * WIN, WIN), F32),
            pltpu.VMEM((3, padded, width_s), BF16),
            pltpu.VMEM((width_t, slots), BF16),
            pltpu.VMEM((width_t, extended), BF16),
            pltpu.VMEM((HEADS * (HD_T + TAIL), extended), BF16),
            pltpu.VMEM((padded, slots), BF16),
            pltpu.VMEM((2, padded, extended), BF16),
            pltpu.VMEM((width_t, slots), BF16),
            pltpu.VMEM((padded, slots), F32),
            pltpu.VMEM((2, windows, 2, 2 * WIN, WIN), BF16),
            pltpu.VMEM((2, windows, 2, 2 * WIN, WIN), BF16),
            pltpu.VMEM((2 * SLOTS, 2 * WIN, WIN), F32),
            pltpu.VMEM((SLOTS, 2 * WIN, WIN), BF16),
            pltpu.SemaphoreType.DMA((4,)),
            pltpu.SemaphoreType.DMA((2, 2)),
            pltpu.SemaphoreType.DMA((2, 2)),
            pltpu.SemaphoreType.DMA((2,)),
            pltpu.SemaphoreType.DMA((4, PAIRS)),
        ],
        compiler_params=pltpu.CompilerParams(
            vmem_limit_bytes=BIG, collective_id=1, has_side_effects=True
        ),
    )(mask, lengths, xt, xs, wtq, wtk, wtv, wq, wk, wv)


def normalize(values, gain, shift):
    n = values.shape[0]
    center = values - jnp.sum(values, axis=0, keepdims=True) * (1.0 / n)
    rscale = lax.rsqrt(jnp.sum(center * center, axis=0, keepdims=True) * (1.0 / n) + EPSILON)
    unit = center * rscale
    return unit * gain + shift, unit, rscale


def normalize_back(grad, unit, rscale, gain):
    n = grad.shape[0]
    scaled = grad * gain
    first = jnp.sum(scaled, axis=0, keepdims=True) * (1.0 / n)
    second = jnp.sum(scaled * unit, axis=0, keepdims=True) * (1.0 / n)
    return rscale * (scaled - first - unit * second)


def fold_lanes(values):
    total = values[:, :128]
    for at in range(128, values.shape[1], 128):
        total = total + values[:, at : at + 128]
    return total


ROOT_HALF = 0.7071067811865476
ROOT_PI = 0.3989422804014327


def dense_kernel(
    inner_pad,
    xt_ref,
    tctx_ref,
    xs_ref,
    sctx_ref,
    stats_ref,
    rows_ref,
    loss_ref,
    vec_t_ref,
    vec_s_ref,
    vec_b_ref,
    two_ref,
    tin_ref,
    tout_ref,
    wo_ref,
    w1_ref,
    w2_ref,
    wh_ref,
    out_ref,
    dctx_ref,
    dres_ref,
    pack_ref,
    ghid_ref,
    gouter_ref,
    ginner_ref,
    gwo_ref,
    gvec_ref,
    col_t_ref,
    col_s_ref,
    col_b_ref,
    wop_ref,
    act_ref,
    slope_ref,
):
    step = pl.program_id(0)
    width_s, units_s = w1_ref.shape
    width_t, units_t = tin_ref.shape
    tile = xt_ref.shape[0]

    @pl.when(step == 0)
    def _():
        col_t_ref[...] = jnp.transpose(vec_t_ref[...])
        col_s_ref[...] = jnp.transpose(vec_s_ref[...])
        col_b_ref[...] = jnp.transpose(vec_b_ref[...])
        wop_ref[...] = nn(pad_heads(), wo_ref[...]).astype(BF16)
        ghid_ref[...] = jnp.zeros_like(ghid_ref)
        gouter_ref[...] = jnp.zeros_like(gouter_ref)
        ginner_ref[...] = jnp.zeros_like(ginner_ref)
        gwo_ref[...] = jnp.zeros_like(gwo_ref)
        gvec_ref[...] = jnp.zeros_like(gvec_ref)
        act_ref[units_s:, :] = jnp.ones((inner_pad - units_s, tile), BF16)

    col_t = lambda k: col_t_ref[:, k : k + 1]
    col_s = lambda k: col_s_ref[:, k : k + 1]
    start = jnp.transpose(xt_ref[...]).astype(F32) + tn(two_ref[...], tctx_ref[...])
    t_normed = normalize(start, col_t(0), col_t(1))[0]
    t_low = t_normed.astype(BF16)
    t_sum = t_normed
    for at in range(0, units_t, width_t):
        pre = tn(tin_ref[:, at : at + width_t], t_low)
        active = (0.5 * pre * (1.0 + lax.erf(pre * ROOT_HALF))).astype(BF16)
        t_sum = t_sum + tn(tout_ref[at : at + width_t, :], active)
    target = normalize(t_sum, col_t(2), col_t(3))[0]
    gain_one, shift_one, b_outer, gain_two, shift_two = (col_s(k) for k in range(5))
    context = sctx_ref[...]
    context_low = context.astype(BF16)
    normed, unit_one, rscale_one = normalize(
        xs_ref[...].astype(F32) + tn(wop_ref[...], context_low), gain_one, shift_one
    )
    normed_low = normed.astype(BF16)
    pre = tn(w1_ref[...], normed_low) + col_b_ref[:, 0:1]
    half = 0.5 * (1.0 + lax.erf(pre * ROOT_HALF))
    slope_ref[...] = half + pre * (ROOT_PI * jnp.exp(-0.5 * pre * pre))
    act_ref[:units_s, :] = (pre * half).astype(BF16)
    student, unit_two, rscale_two = normalize(
        normed + nn(w2_ref[...], act_ref[:units_s, :]) + b_outer, gain_two, shift_two
    )
    student_low = student.astype(BF16)
    out_ref[...] = student_low
    gap = tn(wh_ref[...], student_low) - target
    filled = rows_ref[2:3, :]
    masked = filled * gap
    d_proj = (2.0 * masked).astype(BF16)
    ghid_ref[...] += nt(student_low, d_proj)
    d_student = nn(wh_ref[...], d_proj)
    d_two = normalize_back(d_student, unit_two, rscale_two, gain_two)
    d_outer = d_two.astype(BF16)
    gouter_ref[...] += nt(d_outer, act_ref[...])
    d_inner = (tn(w2_ref[...], d_outer) * slope_ref[...]).astype(BF16)
    ones = jnp.ones((8, tile), BF16)
    ginner_ref[:width_s, :units_s] += nt(normed_low, d_inner)
    ginner_ref[width_s:, :units_s] += nt(ones, d_inner)
    d_normed = nn(w1_ref[...], d_inner) + d_two
    d_one = normalize_back(d_normed, unit_one, rscale_one, gain_one)
    dres_ref[...] = d_one
    d_att = d_one.astype(BF16)
    gwo_ref[...] += nt(context_low, d_att)
    d_context = nn(wop_ref[...], d_att)
    row = lax.broadcasted_iota(jnp.int32, (PAD, tile), 0)
    for head in range(HEADS):
        pair, h = head // 2, head % 2
        inverse = stats_ref[pair, h : h + 1, :]
        cross = stats_ref[pair, 2 + h : 3 + h, :]
        rows = slice(head * PAD, (head + 1) * PAD)
        low = (d_context[rows] * inverse).astype(BF16).astype(F32)
        delta = -jnp.sum(low * context[rows], axis=0, keepdims=True) - inverse * cross
        high = delta.astype(BF16).astype(F32)
        rest = delta - high
        middle = rest.astype(BF16).astype(F32)
        low = jnp.where(row == SLOT_ONE, high, low)
        low = jnp.where(row == SLOT_ONE + 1, middle, low)
        low = jnp.where(row == SLOT_ONE + 2, rest - middle, low)
        dctx_ref[rows, :] = low.astype(BF16)
    for k, values in enumerate((d_normed * unit_one, d_normed, d_student * unit_two, d_student)):
        gvec_ref[:width_s, k * 128 : (k + 1) * 128] += fold_lanes(values)
    square = fold_lanes(masked * gap)
    gvec_ref[width_s : width_s + 8, :128] += jnp.sum(square.reshape(-1, 8, 128), axis=0)

    @pl.when(step == pl.num_programs(0) - 1)
    def _():
        low = lambda v: v.astype(BF16)
        pack_ref[...] = jnp.zeros_like(pack_ref)
        pack_ref[:width_s, :] = low(gouter_ref[...])
        pack_ref[BLOCK : BLOCK + width_s + 8, :] = low(ginner_ref[...])
        pack_ref[2 * BLOCK : 2 * BLOCK + width_s, :width_t] = low(ghid_ref[...])
        pack_ref[2 * BLOCK : 2 * BLOCK + width_s, width_t : width_t + width_s] = low(
            tn(pad_heads(), low(gwo_ref[...]))
        )
        lane = lax.broadcasted_iota(jnp.int32, (width_s, 128), 1)
        sums = jnp.zeros((width_s, 128), F32)
        for k in range(4):
            total = jnp.sum(gvec_ref[:width_s, k * 128 : (k + 1) * 128], axis=1, keepdims=True)
            sums = jnp.where(lane == k, total, sums)
        pack_ref[2 * BLOCK : 2 * BLOCK + width_s, SUMS_AT : SUMS_AT + 128] = low(sums)
        square = gvec_ref[width_s : width_s + 8, :128]
        row = lax.broadcasted_iota(jnp.int32, (8, 128), 0)
        for c in range(loss_ref.shape[1] // 128):
            square += jnp.where(row == c % 8, width_t * loss_ref[0:1, c * 128 : (c + 1) * 128], 0.0)
        pack_ref[2 * BLOCK + width_s : 2 * BLOCK + width_s + 8, :128] = low(square)


def dense(packed_rows, xt, tctx, xs, sctx, stats, rows, loss_rows, vec_t, vec_s, vec_b, two, tin, tout, wo, w1, w2, wh):
    slots, width_t = xt.shape
    width_s, units_s = w1.shape
    tile = 2 * WIN
    padded = HEADS * PAD
    inner_pad = -(-units_s // 128) * 128
    once = lambda a: pl.BlockSpec(a.shape, lambda i: (0,) * a.ndim, pipeline_mode=pl.Buffered(1))
    tiled = lambda n: pl.BlockSpec((n, tile), lambda i: (0, i))
    fixed = lambda *shape: pl.BlockSpec(shape, lambda i: (0,) * len(shape))
    sds = jax.ShapeDtypeStruct
    gshapes = [
        (width_s, width_t),
        (width_s, inner_pad),
        (width_s + 8, inner_pad),
        (padded, width_s),
        (width_s + 8, 512),
    ]
    return pl.pallas_call(
        partial(dense_kernel, inner_pad),
        grid=(slots // tile,),
        out_shape=[
            sds((width_s, slots), BF16),
            sds((padded, slots), BF16),
            sds((width_s, slots), F32),
            sds((packed_rows, inner_pad), BF16),
        ],
        in_specs=[
            pl.BlockSpec((tile, width_t), lambda i: (i, 0)),
            tiled(width_t),
            tiled(width_s),
            tiled(padded),
            pl.BlockSpec((PAIRS, 8, tile), lambda i: (0, 0, i)),
            tiled(8),
        ]
        + [once(a) for a in (loss_rows, vec_t, vec_s, vec_b, two, tin, tout, wo, w1, w2, wh)],
        out_specs=[tiled(width_s), tiled(padded), tiled(width_s), fixed(packed_rows, inner_pad)],
        scratch_shapes=[pltpu.VMEM(g, F32) for g in gshapes]
        + [
            pltpu.VMEM((width_t, 8), F32),
            pltpu.VMEM((width_s, 8), F32),
            pltpu.VMEM((units_s, 8), F32),
            pltpu.VMEM((padded, width_s), BF16),
            pltpu.VMEM((inner_pad, tile), BF16),
            pltpu.VMEM((units_s, tile), F32),
        ],
        compiler_params=pltpu.CompilerParams(vmem_limit_bytes=BIG, dimension_semantics=("arbitrary",)),
    )(xt, tctx, xs, sctx, stats, rows, loss_rows, vec_t, vec_s, vec_b, two, tin, tout, wo, w1, w2, wh)


def group_sizes():
    seq = lax.axis_size("seq")
    core = 2 if seq % 2 == 0 else 1
    chain = 4 if seq // core % 4 == 0 else 1
    return {"core": core, "batch": lax.axis_size("batch"), "chain": chain, "outer": seq // core // chain}


class Group:
    def __init__(self, name):
        batch, seq = lax.axis_index("batch"), lax.axis_index("seq")
        sizes = group_sizes()
        self.size = sizes[name]
        if name == "batch":
            self.place = batch
            self.device = lambda j: (j, seq)
        else:
            stride = {"core": 1, "chain": sizes["core"], "outer": sizes["core"] * sizes["chain"]}[name]
            self.place = seq // stride % self.size
            self.device = lambda j: (batch, seq + (j - self.place) * stride)

    def other(self, k):
        return (self.place + k) % self.size


class Chain:
    def __init__(self, names, source, scratch):
        self.names, self.source = names, source
        self.groups = [Group(n) for n in names]
        count = len(names)
        self.outer = Group("outer")
        self.received, self.sums = scratch[:count], scratch[count : 2 * count]
        self.around, self.whole, self.send, self.arrive = scratch[2 * count :]
        rows = self.whole.shape[0]
        self.rows, self.base, base = [], [], 0
        for g in self.groups:
            self.base.append(base)
            rows //= g.size
            base = base + g.place * rows
            self.rows.append(rows)
        self.mine = base
        self.sem = 0
        self.pending = []

    @staticmethod
    def scratch(names, rows, lanes):
        received, sums, copies = [], [], 0
        total, sizes = rows, group_sizes()
        for size in (sizes[n] for n in names):
            rows = rows // size
            received.append(pltpu.VMEM((max(size - 1, 1), rows, lanes), BF16))
            sums.append(pltpu.VMEM((rows, lanes), BF16))
            copies += 2 * (size - 1)
        copies = max(copies + sizes["outer"] - 1, 1)
        return (
            received
            + sums
            + [
                pltpu.VMEM((max(sizes["outer"] - 1, 1), rows, lanes), BF16),
                pltpu.VMEM((total, lanes), BF16),
                pltpu.SemaphoreType.DMA((copies,)),
                pltpu.SemaphoreType.DMA((copies,)),
            ]
        )

    def copy(self, ends):
        at = self.sem
        self.sem += 1

        def form():
            source, target, device = ends()
            return pltpu.make_async_remote_copy(
                src_ref=source,
                dst_ref=target,
                send_sem=self.send.at[at],
                recv_sem=self.arrive.at[at],
                device_id=device,
                device_id_type=MESH,
            )

        form().start()
        self.pending.append(form)

    def scatter(self, k):
        g, rows = self.groups[k], self.rows[k]
        source = self.source if k == 0 else self.sums[k - 1]

        def ends(step):
            other = g.other(step)
            there = pl.ds(pl.multiple_of(other * rows, 16), rows)
            return source.at[there], self.received[k].at[step - 1], g.device(other)

        for step in range(1, g.size):
            self.copy(partial(ends, step))

    def wait(self):
        for form in self.pending:
            form().wait()
        self.pending = []

    def add(self, k):
        self.wait()
        g, rows = self.groups[k], self.rows[k]
        source = self.source if k == 0 else self.sums[k - 1]
        total = source[pl.ds(pl.multiple_of(g.place * rows, 16), rows), :].astype(F32)
        for step in range(1, g.size):
            total = total + self.received[k][step - 1].astype(F32)
        total = total.astype(BF16)
        if k < len(self.groups) - 1 or self.outer.size > 1:
            self.sums[k][...] = total
        if k == len(self.groups) - 1:
            if self.outer.size > 1:
                total = self.exchange(total)
            self.whole[pl.ds(pl.multiple_of(self.mine, 16), rows), :] = total

    def exchange(self, total):
        g = self.outer

        def ends(step):
            return self.sums[-1], self.around.at[step - 1], g.device(g.other(step))

        for step in range(1, g.size):
            self.copy(partial(ends, step))
        self.wait()
        total = total.astype(F32)
        for step in range(1, g.size):
            total = total + self.around[step - 1].astype(F32)
        return total.astype(BF16)

    def gather(self, k):
        g, rows = self.groups[k], self.rows[k]

        def ends(step):
            here = self.whole.at[pl.ds(pl.multiple_of(self.base[k] + g.place * rows, 16), rows)]
            return here, here, g.device(g.other(step))

        for step in range(1, g.size):
            self.copy(partial(ends, step))

    def advance(self, stage):
        count = len(self.groups)
        if 0 < stage <= count:
            self.add(stage - 1)
        else:
            self.wait()
        if stage < count:
            self.scatter(stage)
        elif stage < 2 * count:
            self.gather(2 * count - 1 - stage)


CHAINS = ((0, 896, ("core", "batch", "chain")), (896, 1280, ("core", "chain", "batch")))
LATE = ("core", "batch", "chain")


def back_kernel(
    windows,
    sq_ref,
    skv_ref,
    dctx_ref,
    e_ref,
    g_ref,
    rows_ref,
    pack_ref,
    xs_ref,
    dres_ref,
    wq_ref,
    wk_ref,
    wv_ref,
    dx_ref,
    early_ref,
    late_ref,
    dq_ref,
    dkv_ref,
    give_ref,
    take_ref,
    qkv_ref,
    halo_send,
    halo_arrive,
    out_sem,
    *scratch,
):
    step = pl.program_id(0)
    w = (windows - step) % windows
    slots = windows * WIN
    width_s = xs_ref.shape[0]
    batch, seq = lax.axis_index("batch"), lax.axis_index("seq")
    peers = lax.axis_size("seq")
    chains, used = [], 0
    for first, last, names in CHAINS:
        size = 2 * len(names) + 4
        chains.append(Chain(names, pack_ref.at[:, first:last], scratch[used : used + size]))
        used += size
    late = Chain(LATE, qkv_ref, scratch[used:])
    first_seq, last_seq = seq == 0, seq == peers - 1

    def halo(side):
        return pltpu.make_async_remote_copy(
            src_ref=give_ref.at[side],
            dst_ref=take_ref.at[1 - side],
            send_sem=halo_send.at[side],
            recv_sem=halo_arrive.at[1 - side],
            device_id=(batch, seq - 1 + 2 * side),
            device_id_type=MESH,
        )

    @pl.when(step == 0)
    def _():
        dkv_ref[...] = jnp.zeros_like(dkv_ref)
        take_ref[...] = jnp.zeros_like(take_ref)
        qkv_ref[...] = jnp.zeros_like(qkv_ref)
        barrier = pltpu.get_barrier_semaphore()
        count = 0
        for g in (Group(n) for n in LATE + ("outer",)):
            for k in range(1, g.size):
                pl.semaphore_signal(barrier, inc=1, device_id=g.device(g.other(k)), device_id_type=MESH)
                count += 1

        for move in (1, peers - 1):
            pl.semaphore_signal(
                barrier, inc=1, device_id=(batch, (seq + move) % peers), device_id_type=MESH
            )
        pl.semaphore_wait(barrier, count + 2)

        for c in chains:
            c.advance(0)

    at = pl.multiple_of(w * WIN, WIN)
    left = pl.ds(at, WIN)
    own = pl.ds(pl.multiple_of(at + WIN, WIN), WIN)
    right = pl.ds(pl.multiple_of(at + 2 * WIN, WIN), WIN)
    early_row, late_row = rows_ref[0:1, left], rows_ref[1:2, left]
    early_low, late_low = early_row.astype(BF16), late_row.astype(BF16)

    def one_head(head):
        rows = pl.ds(pl.multiple_of(head * PAD, PAD), PAD)
        query, grad = sq_ref[rows, left], dctx_ref[rows, left]
        stacked = lambda a: jnp.concatenate([a * early_low, a * late_low], axis=0)
        query_fold, grad_fold = stacked(query), stacked(grad)
        beside = lambda k: jnp.concatenate([skv_ref[k, rows, left], skv_ref[k, rows, right]], axis=0)
        keys_fold, values_fold = beside(0), beside(1)
        keys, values = skv_ref[0, rows, own], skv_ref[1, rows, own]
        e_own, e_side = e_ref[0, head, :WIN, :], e_ref[0, head, WIN:, :]
        d_own = (e_own.astype(F32) * (tn(values, grad) + g_ref[0, head, :WIN, :].astype(F32))).astype(BF16)
        d_side = (
            e_side.astype(F32) * (tn(values_fold, grad_fold) + g_ref[0, head, WIN:, :].astype(F32))
        ).astype(BF16)
        side = nn(keys_fold, d_side)
        d_query = nn(keys, d_own) + early_row * side[:PAD] + late_row * side[PAD:]
        dq_ref[rows, left] = (d_query * HD_S**-0.5).astype(BF16)
        for k, (a, a_fold, b, b_fold, scale) in enumerate(
            ((query, query_fold, d_own, d_side, 1.0 / LOG2E), (grad, grad_fold, e_own, e_side, None))
        ):
            fix = (lambda v: v * scale) if scale else (lambda v: v)
            side = fix(nt(a_fold, b_fold))
            dkv_ref[k, rows, own] += fix(nt(a, b))
            dkv_ref[k, rows, left] += side[:PAD]
            dkv_ref[k, rows, right] += side[PAD:]

    def body(pair, carry):
        one_head(2 * pair)
        one_head(2 * pair + 1)
        return carry

    def send_halo():
        for side, lanes in ((0, slice(0, WIN)), (1, slice(WIN + slots, 2 * WIN + slots))):
            give_ref[side] = dkv_ref[:, :, lanes].astype(BF16)

        @pl.when(jnp.logical_not(first_seq))
        def _():
            halo(0).start()

        @pl.when(jnp.logical_not(last_seq))
        def _():
            halo(1).start()

    def advance(stage):
        def run():
            for c in chains:
                c.advance(stage)

        return run

    half = PAIRS // 2
    plan = {(0, 0): [advance(1)], (1, 1): [advance(2), send_halo], (2, 1): [advance(3)], (3, 1): [advance(4)]}
    for part in range(2):
        lax.fori_loop(part * half, (part + 1) * half, body, 0)
        for k in range(windows):
            for action in plan.get((k, part), []):
                pl.when(step == k)(action)

    @pl.when(step == windows - 1)
    def _():
        @pl.when(jnp.logical_not(first_seq))
        def _():
            halo(0).wait_send()
            halo(1).wait_recv()

        @pl.when(jnp.logical_not(last_seq))
        def _():
            halo(1).wait_send()
            halo(0).wait_recv()

        spot = pad_heads()
        plains = []
        for k in range(3):
            if k == 0:
                grad = dq_ref[...]
            else:
                mine = dkv_ref[k - 1, :, WIN : WIN + slots]
                first = mine[:, :WIN] + take_ref[0, k - 1].astype(F32)
                last = mine[:, slots - WIN :] + take_ref[1, k - 1].astype(F32)
                grad = jnp.concatenate([first, mine[:, WIN : slots - WIN], last], axis=1).astype(BF16)
            plain = tn(spot, grad).astype(BF16)
            plains.append(plain)
            qkv_ref[k * BLOCK : k * BLOCK + width_s, :width_s] = nt(xs_ref[...], plain).astype(BF16)
        late.advance(0)
        total = dres_ref[...]
        for w_ref, plain in zip((wq_ref, wk_ref, wv_ref), plains):
            total = total + nn(w_ref[...], plain)
        dx_ref[...] = total.astype(BF16)
        late.advance(1)
        for c in chains:
            c.advance(5)
        late.advance(2)
        late.advance(3)
        for c in chains:
            c.advance(6)
        copies = [
            pltpu.make_async_copy(c.whole, early_ref.at[:, first:last], out_sem.at[n])
            for n, (c, (first, last, _)) in enumerate(zip(chains, CHAINS))
        ]
        for c in copies:
            c.start()
        late.advance(4)
        late.advance(5)
        late.advance(6)
        copies.append(pltpu.make_async_copy(late.whole, late_ref, out_sem.at[len(chains)]))
        copies[-1].start()
        for c in copies:
            c.wait()


def back(sq, skv, dctx, e, g, rows, pack, xs, dres, wq, wk, wv):
    padded, slots = sq.shape
    windows = slots // WIN
    width_s = xs.shape[0]
    packed_rows = pack.shape[0]
    whole = lambda a: pl.BlockSpec(a.shape, lambda i: (0,) * a.ndim, pipeline_mode=pl.Buffered(1))
    saved = pl.BlockSpec((1, HEADS, 2 * WIN, WIN), lambda i: ((windows - i) % windows, 0, 0, 0))
    anywhere = pl.BlockSpec(memory_space=pl.ANY)
    scratch = [
        pltpu.VMEM((padded, slots), BF16),
        pltpu.VMEM((2, padded, slots + 2 * WIN), F32),
        pltpu.VMEM((2, 2, padded, WIN), BF16),
        pltpu.VMEM((2, 2, padded, WIN), BF16),
        pltpu.VMEM((packed_rows, QKV_LANES), BF16),
        pltpu.SemaphoreType.DMA((2,)),
        pltpu.SemaphoreType.DMA((2,)),
        pltpu.SemaphoreType.DMA((len(CHAINS) + 1,)),
    ]
    for first, last, names in CHAINS:
        scratch += Chain.scratch(names, packed_rows, last - first)
    scratch += Chain.scratch(LATE, packed_rows, QKV_LANES)
    return pl.pallas_call(
        partial(back_kernel, windows),
        grid=(windows,),
        out_shape=[
            jax.ShapeDtypeStruct((width_s, slots), BF16),
            jax.ShapeDtypeStruct(pack.shape, BF16),
            jax.ShapeDtypeStruct((packed_rows, QKV_LANES), BF16),
        ],
        in_specs=[whole(sq), whole(skv), whole(dctx), saved, saved]
        + [whole(a) for a in (rows, pack, xs, dres, wq, wk, wv)],
        out_specs=[pl.BlockSpec((width_s, slots), lambda i: (0, 0)), anywhere, anywhere],
        scratch_shapes=scratch,
        compiler_params=pltpu.CompilerParams(
            vmem_limit_bytes=BIG,
            dimension_semantics=("arbitrary",),
            collective_id=0,
            has_side_effects=True,
        ),
    )(sq, skv, dctx, e, g, rows, pack, xs, dres, wq, wk, wv)


def unpack_kernel(
    every,
    width_t,
    early_ref,
    late_ref,
    dx_in_ref,
    dx_ref,
    loss_ref,
    gq_ref,
    gk_ref,
    gv_ref,
    gwo_ref,
    ginner_ref,
    gouter_ref,
    ghid_ref,
    rows_ref,
    binner_ref,
):
    width_s = gq_ref.shape[0]
    units = binner_ref.shape[1]
    scale = 1.0 / every
    full = lambda v: v.astype(F32) * scale
    dx_ref[...] = dx_in_ref[...]
    for k, ref in enumerate((gq_ref, gk_ref, gv_ref)):
        ref[...] = full(late_ref[k * BLOCK : k * BLOCK + width_s, :width_s])
    gouter_ref[...] = full(early_ref[:width_s, :units])
    ginner_ref[...] = full(early_ref[BLOCK : BLOCK + width_s, :units])
    third = slice(2 * BLOCK, 2 * BLOCK + width_s)
    ghid_ref[...] = full(early_ref[third, :width_t])
    gwo_ref[...] = full(early_ref[third, width_t : width_t + width_s])
    binner_ref[...] = full(early_ref[BLOCK + width_s : BLOCK + width_s + 8, :units])[0:1]
    last = units // 128 * 128
    lane = lax.broadcasted_iota(jnp.int32, (width_s, 128), 1)
    columns = jnp.where(
        lane < 4,
        full(early_ref[third, SUMS_AT : SUMS_AT + 128]),
        full(early_ref[:width_s, last : last + 128]),
    )
    rows_ref[...] = jnp.transpose(columns)
    part = early_ref[2 * BLOCK + width_s : 2 * BLOCK + width_s + 8, :128].astype(F32)
    total = jnp.sum(jnp.sum(part, axis=0, keepdims=True), axis=1, keepdims=True)
    loss_ref[...] = total * (scale / width_t)


def unpack(every, width_t, units, early, late, dx):
    width_s = dx.shape[0]
    sds = lambda *shape: jax.ShapeDtypeStruct(shape, F32)
    shapes = [
        jax.ShapeDtypeStruct(dx.shape, BF16),
        sds(1, 1),
        sds(width_s, width_s),
        sds(width_s, width_s),
        sds(width_s, width_s),
        sds(width_s, width_s),
        sds(width_s, units),
        sds(width_s, units),
        sds(width_s, width_t),
        sds(128, width_s),
        sds(1, units),
    ]
    return pl.pallas_call(
        partial(unpack_kernel, every, width_t),
        out_shape=shapes,
        in_specs=[VMEM] * 3,
        out_specs=[VMEM] * len(shapes),
        compiler_params=pltpu.CompilerParams(vmem_limit_bytes=BIG),
    )(early, late, dx)


def local(
    inputs,
    teacher_input,
    filled_slot_mask,
    seg_lengths,
    query_weight,
    key_weight,
    value_weight,
    w_output,
    gain_one,
    shift_one,
    w_inner,
    b_inner,
    w_outer,
    b_outer,
    gain_two,
    shift_two,
    w_hidden,
    teacher_query_weight,
    teacher_key_weight,
    teacher_value_weight,
    teacher_output,
    teacher_gain_one,
    teacher_shift_one,
    teacher_inner,
    teacher_outer,
    teacher_gain_two,
    teacher_shift_two,
):
    xs = jnp.transpose(inputs[0])
    xt = teacher_input[0]
    slots, width_t = xt.shape
    width_s = xs.shape[0]
    units_s = w_inner.shape[1]
    stats, loss_rows, rows, tctx, sctx, sq, skv, e, g = attend(
        filled_slot_mask,
        seg_lengths,
        xt,
        xs,
        teacher_query_weight,
        teacher_key_weight,
        teacher_value_weight,
        query_weight,
        key_weight,
        value_weight,
    )
    fill = lambda n, *rows: jnp.concatenate([jnp.stack(rows), jnp.zeros((8 - len(rows), n), F32)])
    vec_t = fill(width_t, teacher_gain_one, teacher_shift_one, teacher_gain_two, teacher_shift_two)
    vec_s = fill(width_s, gain_one, shift_one, b_outer, gain_two, shift_two)
    vec_b = fill(units_s, b_inner)
    devices = lax.axis_size("seq") * lax.axis_size("batch")
    sizes = group_sizes()
    unit = 16 * sizes["core"] * sizes["batch"] * sizes["chain"]
    packed_rows = -(-3 * BLOCK // unit) * unit
    out, dctx, dres, pack = dense(
        packed_rows,
        xt,
        tctx,
        xs,
        sctx,
        stats,
        rows,
        loss_rows,
        vec_t,
        vec_s,
        vec_b,
        teacher_output,
        teacher_inner,
        teacher_outer,
        w_output,
        w_inner,
        jnp.transpose(w_outer),
        w_hidden,
    )
    dx, early, late = back(sq, skv, dctx, e, g, rows, pack, xs, dres, query_weight, key_weight, value_weight)
    dx, loss, gq, gk, gv, gwo, ginner, gouter, ghid, vectors, binner = unpack(
        slots * devices, width_t, units_s, early, late, dx
    )
    return (
        jnp.transpose(out)[None],
        jnp.transpose(dx)[None],
        loss[0, 0],
        gq,
        gk,
        gv,
        gwo,
        vectors[0],
        vectors[1],
        ginner,
        binner[0],
        jnp.transpose(gouter),
        vectors[units_s % 128],
        vectors[2],
        vectors[3],
        ghid,
    )


def solution(mesh):
    row_split = P("batch", "seq", None)
    return jax.shard_map(
        local,
        mesh=mesh,
        in_specs=(row_split, row_split, P("batch", None), P("batch", None)) + (P(),) * 23,
        out_specs=(row_split, row_split) + (P(),) * 14,
        check_vma=False,
    )
```

time: 692 us -> 161 us (0.23)
  matrix products: 314 us -> 0 us
  Pallas kernels: 0 us -> 155 us
  other arithmetic: 147 us -> 1.31 us
  waiting for transfers between devices: 109 us -> 0 us
  blocking collectives: 47 us -> 0 us
  local copies, waits for them, and re-layouts: 39.4 us -> 3.44 us
  between operations: 19.9 us -> 0.89 us
  starting transfers between devices: 10.4 us -> 0 us
    dot_general x43 -> x0, matrix products: 314 us -> none  [the longest x13 69.4 us: matmul(): return jnp.dot(left_side, right_side, preferred_element_type=jnp.float32)]
    pallas_call x0 -> x4, Pallas kernels: none -> 155 us  [the longest x1 70.9 us: back(): pl.pallas_call(partial(back_kernel, windows), grid=(windows,), out_shape=...]
    psum x1 -> x0, waiting for transfers between devices: 109 us -> none  [local(): lax.psum((g_w_query, g_w_key, g_w_value, g_w_output, g_gain_one, g_shift_...]
    convert_element_type x1 -> x0, other arithmetic: 57.7 us -> none  [local(): (s_prob * (d_prob - jnp.sum(s_prob * d_prob, -1, keepdims=True))).astype(...]
    psum x1 -> x0, blocking collectives: 47 us -> none  [local(): lax.psum((g_w_query, g_w_key, g_w_value, g_w_output, g_gain_one, g_shift_...]
    reduce_sum x8 -> x0, other arithmetic: 45.8 us -> none  [the longest x2 43.3 us: first_softmax(): row_total = jnp.sum(weights, -1, keepdims=True)]
    slice x4 -> x0, other arithmetic: 20.2 us -> none  [the longest x2 15.6 us: local(): t_parts.append(head_context(t_prob, t_value_all[keys_here], HD_T))]
    reshape x10 -> x0, local copies, waits for them, and re-layouts: 14.3 us -> none  [the longest x8 12.4 us: split_heads(): return rows_in.reshape(rows_in.shape[0], HEADS, head_width)]
  transfers between devices with their start and end apart: 5 -> 0, of which waited for: 2 -> 0; matrix products, arithmetic and copies ran while one was open for 4% -> 0% of each run, Pallas kernels for 0% -> 0%
where the time goes in v1:
time: 161 us
  Pallas kernels  155 us (96%)
  local copies, waits for them, and re-layouts  3.44 us (2%)
    pallas_call x1, Pallas kernels, back(): pl.pallas_call(partial(back_kernel, windows), grid=(windows,), out_shape=...  70.9 us
    pallas_call x1, Pallas kernels, attend(): pl.pallas_call(partial(attend_kernel, windows, row_windows), out_shape=(s...  42.6 us
    pallas_call x1, Pallas kernels, dense(): pl.pallas_call(partial(dense_kernel, inner_pad), grid=(slots // tile,), o...  36.5 us
    pallas_call x1, Pallas kernels, unpack(): pl.pallas_call(partial(unpack_kernel, every, width_t), out_shape=shapes,...  5.08 us

profile of v1, /device:TPU:0, one launch (start us, length us, event | category | flops | bytes accessed | tf_op | source)
XLA Modules:
  0.0 160.7 jit_solution(2626128719564439053)
XLA Ops:
  0.7 0.0 copy-start.1
  0.7 0.0 copy-start.2
  0.7 0.0 copy-start.3
  0.7 0.0 copy-start.4
  0.7 0.0 copy-start.5
  0.7 0.0 copy-start.6
  0.7 0.0 copy-start.7
  0.7 0.0 copy-start.8
  0.7 0.0 copy-start.9
  0.7 0.0 copy-start
  0.8 42.6 %shard_map.378 = (f32[6,8,1024]{2,1,0:T(8,128)}, f32[8,1024]{1,0:T(8,128)}, f32[8,1024]{1,0:T(8,128)}, bf16[768,1024]{1,0:T(8,128)(2,1)}, f32[384,1024]{1,0:T(8,...) custom-call(s32[1,8192]{1,0:T(1,128)} %mask_ref.1, ...), custom_call_target="tpu_custom_call" | custom-call | tf_op jit(solution)/shard_map/pallas_call | solution.py:422
  43.4 0.0 copy-done.1
  43.4 0.0 copy-done.2
  43.4 0.0 copy-done.3
  43.5 0.0 copy-done.4
  43.5 0.6 concatenate.9.vec_t_ref
  44.2 0.0 copy-done.9
  44.2 0.6 concatenate.10.vec_s_ref
  44.9 0.6 concatenate.11.vec_b_ref
  45.5 36.5 %shard_map.379 = (bf16[312,1024]{1,0:T(8,128)(2,1)}, bf16[384,1024]{1,0:T(8,128)(2,1)}, f32[312,1024]{1,0:T(8,128)}, bf16[1024,1280]{1,0:T(8,128)(2,1)}) custom-call(bf16[1024,768]{1,0:T(8,128)(2,1)} %bitcast.14, bf16[768,1024]{1,0:T(8,128)(2,1)} %get-tuple-element.43.tctx_ref, bf16[312,1024]{1,0:T(8,128)(2,1)} %bitcast.16, ...), custom_call_target="tpu_custom_call" | custom-call | tf_op jit(solution)/shard_map/pallas_call | solution.py:652
  82.0 70.9 %shard_map.380 = (bf16[312,1024]{1,0:T(8,128)(2,1)}, bf16[1024,1280]{1,0:T(8,128)(2,1)}, bf16[1024,384]{1,0:T(8,128)(2,1)}) custom-call(bf16[384,1024]{1,0:T(8,128)(2,1)} %get-tuple-element.49.sq_ref, bf16[2,384,1536]{2,1,0:T(8,128)(2,1)} %get-tuple-element.50.skv_ref, bf16[384,1024]{1,0:T(8,128)(2,1)} %get-tuple-element.51.dctx_ref, ...), custom_call_target="tpu_custom_call" | custom-call | tf_op jit(solution)/shard_map/pallas_call | solution.py:1047
  152.8 5.1 %shard_map.381 = (bf16[312,1024]{1,0:T(8,128)(2,1)}, f32[1,1]{1,0:T(1,128)}, f32[312,312]{1,0:T(8,128)}, f32[312,312]{1,0:T(8,128)}, f32[312,312]{1,0:T(8,128)},...) custom-call(bf16[1024,1280]{1,0:T(8,128)(2,1)} %get-tuple-element.56, ...), custom_call_target="tpu_custom_call" | custom-call | tf_op jit(solution)/shard_map/pallas_call | solution.py:1128
  157.9 1.5 slice_reduce_fusion
  159.4 1.3 reduce.2
  (17 shorter events, 0.1 us)
Async XLA Ops:
  0.7 42.7 %copy-start.1 = (f32[768]{0:T(1024)S(1)}, f32[768]{0:T(1024)}, u32[]{:S(2)}) copy-start(f32[768]{0:T(1024)} %param.48) | copy-start | bytes 9220
  0.7 42.8 %copy-start.2 = (f32[768]{0:T(1024)S(1)}, f32[768]{0:T(1024)}, u32[]{:S(2)}) copy-start(f32[768]{0:T(1024)} %param.49) | copy-start | bytes 9220
  0.7 42.8 %copy-start.3 = (f32[768]{0:T(1024)S(1)}, f32[768]{0:T(1024)}, u32[]{:S(2)}) copy-start(f32[768]{0:T(1024)} %param.52) | copy-start | bytes 9220
  0.7 42.8 %copy-start.4 = (f32[768]{0:T(1024)S(1)}, f32[768]{0:T(1024)}, u32[]{:S(2)}) copy-start(f32[768]{0:T(1024)} %param.53) | copy-start | bytes 9220
  0.7 43.4 %copy-start.5 = (f32[312]{0:T(512)S(1)}, f32[312]{0:T(512)}, u32[]{:S(2)}) copy-start(f32[312]{0:T(512)} %param.35) | copy-start | bytes 3748
  0.7 43.4 %copy-start.6 = (f32[312]{0:T(512)S(1)}, f32[312]{0:T(512)}, u32[]{:S(2)}) copy-start(f32[312]{0:T(512)} %param.36) | copy-start | bytes 3748
  0.7 43.4 %copy-start.7 = (f32[312]{0:T(512)S(1)}, f32[312]{0:T(512)}, u32[]{:S(2)}) copy-start(f32[312]{0:T(512)} %param.40) | copy-start | bytes 3748
  0.7 43.4 %copy-start.8 = (f32[312]{0:T(512)S(1)}, f32[312]{0:T(512)}, u32[]{:S(2)}) copy-start(f32[312]{0:T(512)} %param.41) | copy-start | bytes 3748
  0.7 43.5 %copy-start.9 = (f32[312]{0:T(512)S(1)}, f32[312]{0:T(512)}, u32[]{:S(2)}) copy-start(f32[312]{0:T(512)} %param.42) | copy-start | bytes 3748
  0.7 44.1 %copy-start = (f32[1200]{0:T(1024)S(1)}, f32[1200]{0:T(1024)}, u32[]{:S(2)}) copy-start(f32[1200]{0:T(1024)} %param.38) | copy-start | bytes 14404
